TPU v7x, 128 devices: a whole 4x4x4 slice. The times are simulated.
128 devices in a mesh: dp: 16 (over z, y), seq: 8 (over x, core).
Axes of the slice: x: 4, y: 4, z: 4, core: 2. Of those that a mesh axis runs over, the one named last changes fastest.
Arguments:
- tokens: bfloat16 [16, 1024, 1024], P('dp', 'seq'), may hold values from -6 to 6
- counts: int32 [16, 8], P('dp'), may hold values from 1 to 128, 577 in all within a row
- cotangent: bfloat16 [16, 1024, 1024], P('dp', 'seq'), may hold values from -6 to 6
- w_qkv: bfloat16 [2, 1024, 3072], P(None, 'dp'), may hold values from -0.1875 to 0.1875
- w_out: bfloat16 [2, 1024, 1024], P(None, 'dp'), may hold values from -0.75 to 0.75
- w_up: bfloat16 [2, 1024, 4096], P(None, 'dp'), may hold values from -0.1875 to 0.1875
- w_down: bfloat16 [2, 4096, 1024], P(None, 'dp'), may hold values from -0.09375 to 0.09375
- norm_gain: bfloat16 [2, 2, 1024], P(None, None, 'dp'), may hold values from 0.5 to 1.5
- norm_shift: bfloat16 [2, 2, 1024], P(None, None, 'dp'), may hold values from -1.75 to 1.75
- bias_qv: bfloat16 [2, 2048], P(None, 'dp'), may hold values from -1.25 to 1.25
- bias_up: bfloat16 [2, 4096], P(None, 'dp'), may hold values from -3 to 3
- bias_branch: bfloat16 [2, 2, 1024], P(None, None, 'dp'), may hold values from -1.75 to 1.75
Outputs:
- output: bfloat16 [16, 1024, 1024], P('dp', 'seq')
- grad_tokens: bfloat16 [16, 1024, 1024], P('dp', 'seq')
- grad_qkv: float32 [2, 1024, 3072], P(None, 'dp')
- grad_out: float32 [2, 1024, 1024], P(None, 'dp')
- grad_up: float32 [2, 1024, 4096], P(None, 'dp')
- grad_down: float32 [2, 4096, 1024], P(None, 'dp')
- grad_gain: float32 [2, 2, 1024], P(None, None, 'dp')
- grad_shift: float32 [2, 2, 1024], P(None, None, 'dp')
- grad_bias_qv: float32 [2, 2048], P(None, 'dp')
- grad_bias_up: float32 [2, 4096], P(None, 'dp')
- grad_bias_branch: float32 [2, 2, 1024], P(None, None, 'dp')
Inputs may be any that keep to these rules, and one draw needn't show every extreme that they name: counts[i, j] is the number of live tokens of image i in the j-th block of 128 slots, which comes first in that block; each row sums to 577 and its largest entry is 128.
All inputs are finite; a program needn't handle non-finite values.
Results may differ from a plain program's by a relative error of at most 0.018.
Values may be sent and summed in bfloat16 or wider, within the bound.
No kernel may reach another device: no remote copies, remote signals or barrier semaphores. Data moves between devices by JAX's collectives and lax.ppermute only.
A program may use at most 256 MiB of HBM per device.

v0:
```python
import jax
import jax.numpy as jnp
from jax import lax
from jax.sharding import PartitionSpec as P

HEAD_DIM = 64


EPSILON = 1e-06


def normalize(inputs, gain_row, shift_row):
    row_mean = jnp.mean(inputs, axis=-1, keepdims=True)
    centered = inputs - row_mean
    variance = jnp.mean(centered * centered, axis=-1, keepdims=True)
    return centered * lax.rsqrt(variance + EPSILON) * gain_row + shift_row


def gelu_exact(values):
    return jax.nn.gelu(values, approximate=False)


def split_heads(block, heads_here):
    return block.reshape(block.shape[0], heads_here, block.shape[1] // heads_here)


def masked_scores(query_heads, key_heads, validity):
    factor = query_heads.shape[2] ** (-0.5)
    scores = (
        jnp.einsum("qhd,khd->hqk", query_heads, key_heads, preferred_element_type=jnp.float32)
        * factor
    )
    return (jnp.where(validity[None, None, :], scores, -1000000000.0), factor)


def attend_image(queries, key_rows, value_rows, validity, heads_here):
    query_heads = split_heads(queries, heads_here)
    key_heads = split_heads(key_rows, heads_here)
    value_heads = split_heads(value_rows, heads_here)
    scores, factor = masked_scores(query_heads, key_heads, validity)
    row_top = jnp.max(scores, axis=-1, keepdims=True)
    shifted = jnp.exp(scores - row_top)
    row_total = jnp.sum(shifted, axis=-1, keepdims=True)
    attention = (shifted / row_total).astype(jnp.bfloat16)
    mixed_heads = jnp.einsum(
        "hqk,khd->qhd", attention, value_heads, preferred_element_type=jnp.float32
    )
    log_total = (row_top + jnp.log(row_total))[:, :, 0]
    return (mixed_heads.reshape(queries.shape).astype(jnp.bfloat16), log_total)


def attend_back(queries, key_rows, value_rows, validity, log_total, grad_mixed, heads_here):
    query_heads = split_heads(queries, heads_here)
    key_heads = split_heads(key_rows, heads_here)
    value_heads = split_heads(value_rows, heads_here)
    grad_heads = split_heads(grad_mixed, heads_here)
    scores, factor = masked_scores(query_heads, key_heads, validity)
    attention = jnp.exp(scores - log_total[:, :, None])
    grad_attention = jnp.einsum(
        "qhd,khd->hqk", grad_heads, value_heads, preferred_element_type=jnp.float32
    )
    inner = jnp.sum(grad_attention * attention, axis=-1, keepdims=True)
    grad_scores = (attention * (grad_attention - inner)).astype(jnp.bfloat16)
    grad_queries = (
        jnp.einsum("hqk,khd->qhd", grad_scores, key_heads, preferred_element_type=jnp.float32)
        * factor
    )
    grad_keys = (
        jnp.einsum("hqk,qhd->khd", grad_scores, query_heads, preferred_element_type=jnp.float32)
        * factor
    )
    grad_values = jnp.einsum(
        "hqk,qhd->khd",
        attention.astype(jnp.bfloat16),
        grad_heads,
        preferred_element_type=jnp.float32,
    )
    shape = queries.shape
    return (
        grad_queries.reshape(shape).astype(jnp.bfloat16),
        grad_keys.reshape(shape).astype(jnp.bfloat16),
        grad_values.reshape(shape).astype(jnp.bfloat16),
    )


def forward_layer(hidden, weights, validity, images, slot_rows, heads_here):
    qkv_weight, out_weight, up_weight, down_weight, gains, shifts, qv_bias, up_bias, branch_bias = (
        weights
    )
    features = hidden.shape[1]
    gains = gains.astype(jnp.float32)
    shifts = shifts.astype(jnp.float32)
    branch_bias = branch_bias.astype(jnp.float32)
    qv_values = qv_bias.astype(jnp.float32)
    normed = normalize(hidden, gains[0], shifts[0]).astype(jnp.bfloat16)
    packed = jnp.dot(normed, qkv_weight, preferred_element_type=jnp.float32)
    packed = packed + jnp.concatenate(
        [qv_values[:features], jnp.zeros((features,), jnp.float32), qv_values[features:]]
    )
    packed = packed.astype(jnp.bfloat16).reshape(images, slot_rows, 3 * features)
    queries = packed[:, :, :features]
    key_rows = packed[:, :, features : 2 * features]
    value_rows = packed[:, :, 2 * features :]
    queries, key_rows, value_rows = (
        lax.all_to_all(queries, "seq", split_axis=2, concat_axis=1, tiled=True),
        lax.all_to_all(key_rows, "seq", split_axis=2, concat_axis=1, tiled=True),
        lax.all_to_all(value_rows, "seq", split_axis=2, concat_axis=1, tiled=True),
    )
    mixed, log_total = lax.map(
        lambda element: attend_image(element[0], element[1], element[2], element[3], heads_here),
        (queries, key_rows, value_rows, validity),
    )
    mixed_rows = lax.all_to_all(mixed, "seq", split_axis=1, concat_axis=2, tiled=True).reshape(
        -1, features
    )
    middle = (
        hidden
        + jnp.dot(mixed_rows, out_weight, preferred_element_type=jnp.float32)
        + branch_bias[0]
    )
    normed_two = normalize(middle, gains[1], shifts[1]).astype(jnp.bfloat16)
    upward = jnp.dot(normed_two, up_weight, preferred_element_type=jnp.float32) + up_bias.astype(
        jnp.float32
    )
    activated = gelu_exact(upward).astype(jnp.bfloat16)
    result = (
        middle
        + jnp.dot(activated, down_weight, preferred_element_type=jnp.float32)
        + branch_bias[1]
    )
    stored = (hidden, queries, key_rows, value_rows, log_total, mixed_rows, middle, upward)
    return (result, stored)


def backward_layer(gradient, weights, stored, validity, images, slot_rows, heads_here):
    qkv_weight, out_weight, up_weight, down_weight, gains, shifts, qv_bias, up_bias, branch_bias = (
        weights
    )
    hidden, queries, key_rows, value_rows, log_total, mixed_rows, middle, upward = stored
    features = gradient.shape[1]
    gains = gains.astype(jnp.float32)
    shifts = shifts.astype(jnp.float32)
    grad_two = gradient.astype(jnp.bfloat16)
    normed_two, norm_two_back = jax.vjp(normalize, middle, gains[1], shifts[1])
    activated, gelu_back = jax.vjp(gelu_exact, upward)
    grad_downw = jnp.einsum(
        "rf,rd->fd", activated.astype(jnp.bfloat16), grad_two, preferred_element_type=jnp.float32
    )
    grad_bias_two = jnp.sum(grad_two.astype(jnp.float32), axis=0)
    grad_activated = jnp.einsum(
        "rd,fd->rf", grad_two, down_weight, preferred_element_type=jnp.float32
    )
    grad_upward = gelu_back(grad_activated)[0].astype(jnp.bfloat16)
    grad_upw = jnp.einsum(
        "rd,rf->df",
        normed_two.astype(jnp.bfloat16),
        grad_upward,
        preferred_element_type=jnp.float32,
    )
    grad_upb = jnp.sum(grad_upward.astype(jnp.float32), axis=0)
    grad_normed_two = jnp.einsum(
        "rf,df->rd", grad_upward, up_weight, preferred_element_type=jnp.float32
    )
    grad_middle, grad_gain_two, grad_shift_two = norm_two_back(grad_normed_two)
    grad_middle = grad_middle + gradient
    grad_one = grad_middle.astype(jnp.bfloat16)
    grad_outw = jnp.einsum("rd,re->de", mixed_rows, grad_one, preferred_element_type=jnp.float32)
    grad_bias_one = jnp.sum(grad_one.astype(jnp.float32), axis=0)
    grad_mixed = jnp.einsum("re,de->rd", grad_one, out_weight, preferred_element_type=jnp.float32)
    grad_mixed = grad_mixed.astype(jnp.bfloat16).reshape(images, slot_rows, features)
    grad_mixed = lax.all_to_all(grad_mixed, "seq", split_axis=2, concat_axis=1, tiled=True)
    grad_queries, grad_keys, grad_values = lax.map(
        lambda element: attend_back(
            element[0], element[1], element[2], element[3], element[4], element[5], heads_here
        ),
        (queries, key_rows, value_rows, validity, log_total, grad_mixed),
    )
    grad_queries, grad_keys, grad_values = (
        lax.all_to_all(grad_queries, "seq", split_axis=1, concat_axis=2, tiled=True),
        lax.all_to_all(grad_keys, "seq", split_axis=1, concat_axis=2, tiled=True),
        lax.all_to_all(grad_values, "seq", split_axis=1, concat_axis=2, tiled=True),
    )
    grad_packed = jnp.concatenate([grad_queries, grad_keys, grad_values], axis=2).reshape(
        -1, 3 * features
    )
    normed, norm_one_back = jax.vjp(normalize, hidden, gains[0], shifts[0])
    grad_qkvw = jnp.einsum(
        "rd,rc->dc", normed.astype(jnp.bfloat16), grad_packed, preferred_element_type=jnp.float32
    )
    column_sums = jnp.sum(grad_packed.astype(jnp.float32), axis=0)
    grad_qv = jnp.concatenate([column_sums[:features], column_sums[2 * features :]])
    grad_normed = jnp.einsum(
        "rc,dc->rd", grad_packed, qkv_weight, preferred_element_type=jnp.float32
    )
    grad_hidden, grad_gain_one, grad_shift_one = norm_one_back(grad_normed)
    grad_hidden = grad_hidden + grad_middle
    layer_grads = (
        grad_qkvw,
        grad_outw,
        grad_upw,
        grad_downw,
        jnp.stack([grad_gain_one, grad_gain_two]),
        jnp.stack([grad_shift_one, grad_shift_two]),
        grad_qv,
        grad_upb,
        jnp.stack([grad_bias_one, grad_bias_two]),
    )
    return (grad_hidden, layer_grads)


def share_gradients(layer_grads):
    (
        grad_qkvw,
        grad_outw,
        grad_upw,
        grad_downw,
        grad_gains,
        grad_shifts,
        grad_qv,
        grad_upb,
        grad_branch,
    ) = layer_grads
    owned = (
        lax.psum_scatter(
            grad_qkvw.astype(jnp.bfloat16), "dp", scatter_dimension=0, tiled=True
        ).astype(jnp.float32),
        lax.psum_scatter(
            grad_outw.astype(jnp.bfloat16), "dp", scatter_dimension=0, tiled=True
        ).astype(jnp.float32),
        lax.psum_scatter(
            grad_upw.astype(jnp.bfloat16), "dp", scatter_dimension=0, tiled=True
        ).astype(jnp.float32),
        lax.psum_scatter(
            grad_downw.astype(jnp.bfloat16), "dp", scatter_dimension=0, tiled=True
        ).astype(jnp.float32),
        lax.psum_scatter(
            grad_gains.astype(jnp.bfloat16), "dp", scatter_dimension=1, tiled=True
        ).astype(jnp.float32),
        lax.psum_scatter(
            grad_shifts.astype(jnp.bfloat16), "dp", scatter_dimension=1, tiled=True
        ).astype(jnp.float32),
        lax.psum_scatter(
            grad_qv.astype(jnp.bfloat16), "dp", scatter_dimension=0, tiled=True
        ).astype(jnp.float32),
        lax.psum_scatter(
            grad_upb.astype(jnp.bfloat16), "dp", scatter_dimension=0, tiled=True
        ).astype(jnp.float32),
        lax.psum_scatter(
            grad_branch.astype(jnp.bfloat16), "dp", scatter_dimension=1, tiled=True
        ).astype(jnp.float32),
    )
    return (
        lax.psum(owned[0].astype(jnp.bfloat16), "seq").astype(jnp.float32),
        lax.psum(owned[1].astype(jnp.bfloat16), "seq").astype(jnp.float32),
        lax.psum(owned[2].astype(jnp.bfloat16), "seq").astype(jnp.float32),
        lax.psum(owned[3].astype(jnp.bfloat16), "seq").astype(jnp.float32),
        lax.psum(owned[4].astype(jnp.bfloat16), "seq").astype(jnp.float32),
        lax.psum(owned[5].astype(jnp.bfloat16), "seq").astype(jnp.float32),
        lax.psum(owned[6].astype(jnp.bfloat16), "seq").astype(jnp.float32),
        lax.psum(owned[7].astype(jnp.bfloat16), "seq").astype(jnp.float32),
        lax.psum(owned[8].astype(jnp.bfloat16), "seq").astype(jnp.float32),
    )


def shards(
    tokens,
    counts,
    cotangent,
    w_qkv,
    w_out,
    w_up,
    w_down,
    norm_gain,
    norm_shift,
    bias_qv,
    bias_up,
    bias_branch,
):
    images, slot_rows, features = tokens.shape
    seq_count = lax.axis_size("seq")
    heads_here = features // seq_count // HEAD_DIM
    positions = jnp.arange(seq_count * slot_rows, dtype=jnp.int32)
    validity = (positions % slot_rows)[None, :] < jnp.repeat(counts, slot_rows, axis=1)
    seq_index = lax.axis_index("seq")
    local_valid = lax.dynamic_slice_in_dim(validity, seq_index * slot_rows, slot_rows, 1)
    row_mask = local_valid.reshape(-1, 1).astype(jnp.float32)
    layers = w_qkv.shape[0]
    hidden = tokens.reshape(-1, features).astype(jnp.float32)
    fetched = []
    kept = []
    for layer_index in range(layers):
        weights = (
            lax.all_gather(w_qkv[layer_index], "dp", axis=0, tiled=True),
            lax.all_gather(w_out[layer_index], "dp", axis=0, tiled=True),
            lax.all_gather(w_up[layer_index], "dp", axis=0, tiled=True),
            lax.all_gather(w_down[layer_index], "dp", axis=0, tiled=True),
            lax.all_gather(norm_gain[layer_index], "dp", axis=1, tiled=True),
            lax.all_gather(norm_shift[layer_index], "dp", axis=1, tiled=True),
            lax.all_gather(bias_qv[layer_index], "dp", axis=0, tiled=True),
            lax.all_gather(bias_up[layer_index], "dp", axis=0, tiled=True),
            lax.all_gather(bias_branch[layer_index], "dp", axis=1, tiled=True),
        )
        fetched.append(weights)
        hidden, stored = forward_layer(hidden, weights, validity, images, slot_rows, heads_here)
        kept.append(stored)
    output = (hidden * row_mask).astype(jnp.bfloat16).reshape(tokens.shape)
    gradient = cotangent.reshape(-1, features).astype(jnp.float32) * row_mask
    shared = [None] * layers
    for layer_index in reversed(range(layers)):
        weights = (
            lax.all_gather(w_qkv[layer_index], "dp", axis=0, tiled=True),
            lax.all_gather(w_out[layer_index], "dp", axis=0, tiled=True),
            lax.all_gather(w_up[layer_index], "dp", axis=0, tiled=True),
            lax.all_gather(w_down[layer_index], "dp", axis=0, tiled=True),
            lax.all_gather(norm_gain[layer_index], "dp", axis=1, tiled=True),
            lax.all_gather(norm_shift[layer_index], "dp", axis=1, tiled=True),
            lax.all_gather(bias_qv[layer_index], "dp", axis=0, tiled=True),
            lax.all_gather(bias_up[layer_index], "dp", axis=0, tiled=True),
            lax.all_gather(bias_branch[layer_index], "dp", axis=1, tiled=True),
        )
        gradient, layer_grads = backward_layer(
            gradient, weights, kept[layer_index], validity, images, slot_rows, heads_here
        )
        shared[layer_index] = share_gradients(layer_grads)
    grad_tokens = gradient.astype(jnp.bfloat16).reshape(tokens.shape)
    stacked = [
        jnp.stack([shared[layer_index][member] for layer_index in range(layers)], axis=0)
        for member in range(9)
    ]
    return (
        output,
        grad_tokens,
        stacked[0],
        stacked[1],
        stacked[2],
        stacked[3],
        stacked[4],
        stacked[5],
        stacked[6],
        stacked[7],
        stacked[8],
    )


def solution(mesh):
    placed = (
        P("dp", "seq", None),
        P("dp", None),
        P("dp", "seq", None),
        P(None, "dp", None),
        P(None, "dp", None),
        P(None, "dp", None),
        P(None, "dp", None),
        P(None, None, "dp"),
        P(None, None, "dp"),
        P(None, "dp"),
        P(None, "dp"),
        P(None, None, "dp"),
    )
    return jax.shard_map(
        shards,
        mesh=mesh,
        in_specs=placed,
        out_specs=(
            P("dp", "seq", None),
            P("dp", "seq", None),
            P(None, "dp", None),
            P(None, "dp", None),
            P(None, "dp", None),
            P(None, "dp", None),
            P(None, None, "dp"),
            P(None, None, "dp"),
            P(None, "dp"),
            P(None, "dp"),
            P(None, None, "dp"),
        ),
        check_vma=False,
    )
```

profile of v0, /device:TPU:1, one launch (start us, length us, event | category | flops | bytes accessed | tf_op | source)
XLA Modules:
  0.0 1771.9 jit_solution(392055310200003688)
XLA Ops:
  15.3 19.5 %all-gather.12 = bf16[1,2048]{1,0:T(2,128)(2,1)S(1)} all-gather(bf16[1,128]{1,0:T(2,128)(2,1)S(1)} %get-tuple-element.205), channel_id=14, replica_groups=mesh['dp'=16,'seq'=8] {'dp'}, dimensions={1}, use_global_device_ids=true | all-gather | bytes 4352 | tf_op jit(solution)/shard_map/all_gather | solution.py:299
  34.9 15.1 all-gather.3
  50.2 20.1 %all-gather = bf16[1,2,1024]{1,0,2:T(2,128)(2,1)S(1)} all-gather(bf16[1,2,64]{1,0,2:T(2,128)(2,1)S(1)} %copy.215), channel_id=2, replica_groups=mesh['dp'=16,'seq'=8] {'dp'}, dimensions={2}, use_global_device_ids=true | all-gather | bytes 4352 | tf_op jit(solution)/shard_map/all_gather | solution.py:297
  70.9 18.5 %all-gather.1 = bf16[1,2,1024]{1,0,2:T(2,128)(2,1)S(1)} all-gather(bf16[1,2,64]{1,0,2:T(2,128)(2,1)S(1)} %copy.216), channel_id=3, replica_groups=mesh['dp'=16,'seq'=8] {'dp'}, dimensions={2}, use_global_device_ids=true | all-gather | bytes 4352 | tf_op jit(solution)/shard_map/all_gather | solution.py:298
  90.2 6.2 slice_reduce_fusion.8
  96.4 6.2 slice_reduce_fusion.7
  110.9 20.5 %all-to-all-start.2 = ((bf16[8,2,8192]{2,1,0:T(2,128)(2,1)}), bf16[8,2,8192]{2,1,0:T(2,128)(2,1)S(1)}, u32[]{:S(2)}, u32[]{:S(2)}) async-start(bf16[8,2,8192]{2,1,0:T(2,128)(2,1)} %reshape.605), calls=%async_computation.2 | async-start | bytes 524288 | tf_op jit(solution)/shard_map/all_to_all | solution.py:106
  142.4 19.0 %all-gather.5 = bf16[1,2,1024]{1,0,2:T(2,128)(2,1)S(1)} all-gather(bf16[1,2,64]{1,0,2:T(2,128)(2,1)S(1)} %copy.217), channel_id=7, replica_groups=mesh['dp'=16,'seq'=8] {'dp'}, dimensions={2}, use_global_device_ids=true | all-gather | bytes 4352 | tf_op jit(solution)/shard_map/all_gather | solution.py:301
  162.0 6.2 slice_reduce_fusion.6
  171.6 9.1 all-to-all-start
  181.0 19.9 %all-gather.9 = bf16[1,2,1024]{1,0,2:T(2,128)(2,1)S(1)} all-gather(bf16[1,2,64]{1,0,2:T(2,128)(2,1)S(1)} %copy.218), channel_id=11, replica_groups=mesh['dp'=16,'seq'=8] {'dp'}, dimensions={2}, use_global_device_ids=true | all-gather | bytes 4352 | tf_op jit(solution)/shard_map/all_gather | solution.py:297
  201.4 6.2 slice_reduce_fusion.2
  219.3 8.3 all-to-all-start.3
  227.7 17.9 %all-gather.7 = bf16[1,4096]{1,0:T(2,128)(2,1)S(1)} all-gather(bf16[1,256]{1,0:T(2,128)(2,1)S(1)} %get-tuple-element.198), channel_id=9, replica_groups=mesh['dp'=16,'seq'=8] {'dp'}, dimensions={1}, use_global_device_ids=true | all-gather | bytes 8704 | tf_op jit(solution)/shard_map/all_gather | solution.py:300
  245.7 21.1 %all-gather.10 = bf16[1,2,1024]{1,0,2:T(2,128)(2,1)S(1)} all-gather(bf16[1,2,64]{1,0,2:T(2,128)(2,1)S(1)} %copy.219), channel_id=12, replica_groups=mesh['dp'=16,'seq'=8] {'dp'}, dimensions={2}, use_global_device_ids=true | all-gather | bytes 4352 | tf_op jit(solution)/shard_map/all_gather | solution.py:298
  267.4 6.2 slice_reduce_fusion.1
  277.0 9.1 multiply_convert_fusion.3
  286.1 5.4 fusion.221
  291.7 46.8 %all-gather.35.cloned.1.call-done = bf16[1,1024,3072]{2,1,0:T(8,128)(2,1)} async-done(((bf16[1,64,3072]{2,1,0:T(8,128)(2,1)}), bf16[1,1024,3072]{2,1,0:T(8,128)(2,1)}) %all-gather.35.cloned.1.call-update) | async-done | bytes 6291472 | tf_op jit(solution)/shard_map/all_gather | solution.py:293
  345.8 4.9 all-to-all-start.6
  373.9 5.3 all-to-all-done.4
  394.0 19.4 %all-gather.16 = bf16[1,4096]{1,0:T(2,128)(2,1)S(1)} all-gather(bf16[1,256]{1,0:T(2,128)(2,1)S(1)} %get-tuple-element.197), channel_id=18, replica_groups=mesh['dp'=16,'seq'=8] {'dp'}, dimensions={1}, use_global_device_ids=true | all-gather | bytes 8704 | tf_op jit(solution)/shard_map/all_gather | solution.py:300
  413.5 18.8 %all-gather.14 = bf16[1,2,1024]{1,0,2:T(2,128)(2,1)S(1)} all-gather(bf16[1,2,64]{1,0,2:T(2,128)(2,1)S(1)} %copy.220), channel_id=16, replica_groups=mesh['dp'=16,'seq'=8] {'dp'}, dimensions={2}, use_global_device_ids=true | all-gather | bytes 4352 | tf_op jit(solution)/shard_map/all_gather | solution.py:301
  432.9 6.2 slice_reduce_fusion
  442.5 18.1 %all-gather.39.cloned.1.call-done = bf16[1,1024,4096]{2,1,0:T(8,128)(2,1)} async-done(((bf16[1,64,4096]{2,1,0:T(8,128)(2,1)}), bf16[1,1024,4096]{2,1,0:T(8,128)(2,1)}) %all-gather.39.cloned.1.call-update) | async-done | bytes 8388624 | tf_op jit(solution)/shard_map/all_gather | solution.py:295
  460.6 9.1 multiply_convert_fusion.2
  469.8 63.2 %all-gather.41.cloned.1.call-done = bf16[1,4096,1024]{2,1,0:T(8,128)(2,1)} async-done(((bf16[1,256,1024]{2,1,0:T(8,128)(2,1)}), bf16[1,4096,1024]{2,1,0:T(8,128)(2,1)}) %all-gather.41.cloned.1.call-update) | async-done | bytes 8388624 | tf_op jit(solution)/shard_map/all_gather | solution.py:296
  533.0 9.9 fusion.224
  556.9 4.9 all-to-all-start.8
  562.8 5.5 all-to-all-done.8
  572.4 5.6 fusion.123
  577.9 8.2 multiply_reduce_fusion.1
  591.9 5.0 all-to-all-start.11
  596.9 7.1 multiply_convert_fusion.1
  612.0 5.1 all-to-all-start.10
  646.5 5.3 multiply_reduce_fusion.3
  653.5 9.7 fusion.225
  670.6 5.8 convolution_convert_fusion.4
  691.2 6.6 all-to-all-done.12
  699.3 5.5 fusion.120
  712.4 5.2 all-to-all-start.15
  717.7 5.2 multiply_reduce_fusion
  747.4 4.9 all-to-all-start.13
  766.6 5.6 convolution_convert_fusion.5
  772.4 6.9 convolution_convert_fusion.2
  779.4 5.6 convolution_convert_fusion
  786.3 5.7 convolution_convert_fusion.3
  793.2 5.6 convolution_convert_fusion.1
  801.4 5.5 fusion.138
  811.3 5.1 fusion.196
  818.8 57.3 %reduce-scatter.29.cloned.1.call-done = bf16[64,3072]{1,0:T(8,128)(2,1)} async-done(((bf16[1024,3072]{1,0:T(8,128)(2,1)}), bf16[64,3072]{1,0:T(8,128)(2,1)}) %reduce-scatter.29.cloned.1.call-update) | async-done | bytes 393232 | tf_op jit(solution)/shard_map/reduce_scatter | solution.py:224
  876.1 84.7 %reduce-scatter.27.cloned.1.call-done = bf16[64,3072]{1,0:T(8,128)(2,1)} async-done(((bf16[1024,3072]{1,0:T(8,128)(2,1)}), bf16[64,3072]{1,0:T(8,128)(2,1)}) %reduce-scatter.27.cloned.1.call-update) | async-done | bytes 393232 | tf_op jit(solution)/shard_map/reduce_scatter | solution.py:224
  960.8 87.7 %reduce-scatter.37.cloned.1.call-done = bf16[64,4096]{1,0:T(8,128)(2,1)} async-done(((bf16[1024,4096]{1,0:T(8,128)(2,1)}), bf16[64,4096]{1,0:T(8,128)(2,1)}) %reduce-scatter.37.cloned.1.call-update) | async-done | bytes 524304 | tf_op jit(solution)/shard_map/reduce_scatter | solution.py:230
  1048.6 88.1 %reduce-scatter.41.cloned.1.call-done = bf16[256,1024]{1,0:T(8,128)(2,1)} async-done(((bf16[4096,1024]{1,0:T(8,128)(2,1)}), bf16[256,1024]{1,0:T(8,128)(2,1)}) %reduce-scatter.41.cloned.1.call-update) | async-done | bytes 524304 | tf_op jit(solution)/shard_map/reduce_scatter | solution.py:233
  1136.6 88.1 %reduce-scatter.35.cloned.1.call-done = bf16[64,4096]{1,0:T(8,128)(2,1)} async-done(((bf16[1024,4096]{1,0:T(8,128)(2,1)}), bf16[64,4096]{1,0:T(8,128)(2,1)}) %reduce-scatter.35.cloned.1.call-update) | async-done | bytes 524304 | tf_op jit(solution)/shard_map/reduce_scatter | solution.py:230
  1224.7 87.9 %reduce-scatter.39.cloned.1.call-done = bf16[256,1024]{1,0:T(8,128)(2,1)} async-done(((bf16[4096,1024]{1,0:T(8,128)(2,1)}), bf16[256,1024]{1,0:T(8,128)(2,1)}) %reduce-scatter.39.cloned.1.call-update) | async-done | bytes 524304 | tf_op jit(solution)/shard_map/reduce_scatter | solution.py:233
  1312.6 74.2 %reduce-scatter.49.cloned.1.call-done = bf16[64,2]{1,0:T(8,128)(2,1)} async-done(((bf16[1024,2]{1,0:T(8,128)(2,1)}), bf16[64,2]{1,0:T(8,128)(2,1)}) %reduce-scatter.49.cloned.1.call-update) | async-done | bytes 272
  1387.6 74.2 %reduce-scatter.45.cloned.1.call-done = bf16[64,2]{1,0:T(8,128)(2,1)} async-done(((bf16[1024,2]{1,0:T(8,128)(2,1)}), bf16[64,2]{1,0:T(8,128)(2,1)}) %reduce-scatter.45.cloned.1.call-update) | async-done | bytes 272
  1462.6 73.9 %reduce-scatter.51.cloned.1.call-done = bf16[64,2]{1,0:T(8,128)(2,1)} async-done(((bf16[1024,2]{1,0:T(8,128)(2,1)}), bf16[64,2]{1,0:T(8,128)(2,1)}) %reduce-scatter.51.cloned.1.call-update) | async-done | bytes 272
  1537.6 57.9 %all-reduce.4 = (bf16[2048]{0:T(1024)(128)(2,1)S(1)}, bf16[2048]{0:T(1024)(128)(2,1)S(1)}, bf16[4096]{0:T(1024)(128)(2,1)S(1)}, bf16[4096]{0:T(1024)(128)(2,1)S(1)}) all-reduce(bf16[2048]{0:T(1024)(128)(2,1)S(1)} %pad_maximum_fusion.9, bf16[2048]{0:T(1024)(128)(2,1)S(1)} %pad_maximum_fusion.8, ...), channel_id=33, replica_groups=mesh['dp'=16,'seq'=8] {'dp'}, use_global_device_ids=true, to_apply=%region_58.59.clone | all-reduce | flops 12288 | bytes 49152
  1596.7 14.8 reduce-scatter.43.cloned.1.call-done
  1612.3 74.0 %reduce-scatter.47.cloned.1.call-done = bf16[64,2]{1,0:T(8,128)(2,1)} async-done(((bf16[1024,2]{1,0:T(8,128)(2,1)}), bf16[64,2]{1,0:T(8,128)(2,1)}) %reduce-scatter.47.cloned.1.call-update) | async-done | bytes 272
  1687.1 14.3 all-reduce.5
  1704.3 53.6 %all-reduce.9.cloned.1.call-done = (bf16[1,64,3072]{2,1,0:T(8,128)(2,1)}, bf16[1,64,3072]{2,1,0:T(8,128)(2,1)}, bf16[1,64,1024]{2,1,0:T(8,128)(2,1)}, bf16[1,64,...) async-done(((bf16[1,64,3072]{2,1,0:T(8,128)(2,1)}, ...) | async-done | bytes 3145744 | tf_op jit(solution)/shard_map/psum | solution.py:253
  (465 shorter events, 257.7 us)
Async XLA Ops:
  7.2 95.4 %all-gather.27.cloned.1.call-start = ((), (), s32[]{:S(2)}) async-start(), calls=%async_computation.38 | async-start | bytes 6684672 | tf_op jit(solution)/shard_map/all_gather | solution.py:293
  9.4 265.1 %all-gather.29.cloned.1.call-start = ((), (), s32[]{:S(2)}) async-start(), calls=%async_computation.39 | async-start | bytes 2228224 | tf_op jit(solution)/shard_map/all_gather | solution.py:294
  10.2 266.8 %all-gather.31.cloned.1.call-start = ((), (), s32[]{:S(2)}) async-start(), calls=%async_computation.40 | async-start | bytes 8912896 | tf_op jit(solution)/shard_map/all_gather | solution.py:295
  11.4 274.8 %all-gather.33.cloned.1.call-start = ((), (), s32[]{:S(2)}) async-start(), calls=%async_computation.41 | async-start | bytes 8912896 | tf_op jit(solution)/shard_map/all_gather | solution.py:296
  12.5 326.0 %all-gather.35.cloned.1.call-start = ((), (), s32[]{:S(2)}) async-start(), calls=%async_computation.42 | async-start | bytes 6684672 | tf_op jit(solution)/shard_map/all_gather | solution.py:293
  13.1 427.0 %all-gather.37.cloned.1.call-start = ((), (), s32[]{:S(2)}) async-start(), calls=%async_computation.43 | async-start | bytes 2228224 | tf_op jit(solution)/shard_map/all_gather | solution.py:294
  13.7 447.0 %all-gather.39.cloned.1.call-start = ((), (), s32[]{:S(2)}) async-start(), calls=%async_computation.44 | async-start | bytes 8912896 | tf_op jit(solution)/shard_map/all_gather | solution.py:295
  14.4 518.6 %all-gather.41.cloned.1.call-start = ((), (), s32[]{:S(2)}) async-start(), calls=%async_computation.45 | async-start | bytes 8912896 | tf_op jit(solution)/shard_map/all_gather | solution.py:296
  89.9 16.6 copy-start.59
  90.1 16.4 copy-start.68
  90.2 16.4 copy-start.61
  96.4 10.1 copy-start.52
  102.6 174.5 %copy-start.57 = (f32[1024]{0:T(1024)}, f32[1024]{0:T(1024)S(1)}, u32[]{:S(2)}) copy-start(f32[1024]{0:T(1024)S(1)} %get-tuple-element.136) | copy-start | bytes 12292
  107.9 34.4 %copy-start.67 = (bf16[2,2,64]{2,1,0:T(2,128)(2,1)S(1)}, bf16[2,2,64]{2,1,0:T(2,128)(2,1)}, u32[]{:S(2)}) copy-start(bf16[2,2,64]{2,1,0:T(2,128)(2,1)} %param.23) | copy-start | bytes 1540
  110.9 27.0 %all-to-all-start.2 = ((bf16[8,2,8192]{2,1,0:T(2,128)(2,1)}), bf16[8,2,8192]{2,1,0:T(2,128)(2,1)S(1)}, u32[]{:S(2)}, u32[]{:S(2)}) async-start(bf16[8,2,8192]{2,1,0:T(2,128)(2,1)} %reshape.605), calls=%async_computation.2 | async-start | bytes 524288 | tf_op jit(solution)/shard_map/all_to_all | solution.py:106
  137.9 33.7 %all-to-all-start.1 = ((bf16[8,2,8192]{2,1,0:T(2,128)(2,1)}), bf16[8,2,8192]{2,1,0:T(2,128)(2,1)S(1)}, u32[]{:S(2)}, u32[]{:S(2)}) async-start(bf16[8,2,8192]{2,1,0:T(2,128)(2,1)} %reshape.603), calls=%async_computation.1 | async-start | bytes 524288 | tf_op jit(solution)/shard_map/all_to_all | solution.py:105
  162.0 18.8 %copy-start.70 = (s32[1,8]{1,0:T(1,128)S(1)}, s32[1,8]{1,0:T(1,128)}, u32[]{:S(2)}) copy-start(s32[1,8]{1,0:T(1,128)} %param.13) | copy-start | bytes 100
  171.6 37.3 %all-to-all-start = ((bf16[8,2,8192]{2,1,0:T(2,128)(2,1)}), bf16[8,2,8192]{2,1,0:T(2,128)(2,1)S(1)}, u32[]{:S(2)}, u32[]{:S(2)}) async-start(bf16[8,2,8192]{2,1,0:T(2,128)(2,1)} %reshape.601), calls=%async_computation | async-start | bytes 524288 | tf_op jit(solution)/shard_map/all_to_all | solution.py:107
  215.9 11.7 copy-start.63
  219.3 54.2 %all-to-all-start.3 = ((bf16[8,2,8192]{2,1,0:T(2,128)(2,1)}), bf16[8,2,8192]{2,1,0:T(2,128)(2,1)S(1)}, u32[]{:S(2)}, u32[]{:S(2)}) async-start(bf16[8,2,8192]{2,1,0:T(2,128)(2,1)} %reshape.607), calls=%async_computation.3 | async-start | bytes 524288 | tf_op jit(solution)/shard_map/all_to_all | solution.py:113
  274.5 11.6 copy-start.40
  345.8 11.4 all-to-all-start.6
  357.2 11.0 all-to-all-start.5
  368.3 10.9 all-to-all-start.4
  389.6 49.6 %all-to-all-start.7 = ((bf16[8,2,8192]{2,1,0:T(2,128)(2,1)}), bf16[8,2,8192]{2,1,0:T(2,128)(2,1)S(1)}, u32[]{:S(2)}, u32[]{:S(2)}) async-start(bf16[8,2,8192]{2,1,0:T(2,128)(2,1)} %reshape.615), calls=%async_computation.7 | async-start | bytes 524288 | tf_op jit(solution)/shard_map/all_to_all | solution.py:113
  440.0 20.6 %copy-start.39 = (bf16[1,128,8,128]{1,3,2,0:T(8,128)(2,1)}, bf16[1,128,8,128]{1,3,2,0:T(8,128)(2,1)S(1)}, u32[]{:S(2)}) copy-start(bf16[1,128,8,128]{1,3,2,0:T(8,128)(2,1)S(1)} %copy.155) | copy-start | bytes 786436
  460.6 72.3 %copy-start.21 = (bf16[1,128,1024]{2,1,0:T(8,128)(2,1)S(1)}, bf16[1,128,1024]{2,1,0:T(8,128)(2,1)}, u32[]{:S(2)}) copy-start(bf16[1,128,1024]{2,1,0:T(8,128)(2,1)} %param.14) | copy-start | bytes 786436
  469.8 309.6 %copy-start.8 = (bf16[128,4096]{1,0:T(8,128)(2,1)}, bf16[128,4096]{1,0:T(8,128)(2,1)S(1)}, u32[]{:S(2)}) copy-start(bf16[128,4096]{1,0:T(8,128)(2,1)S(1)} %get-tuple-element.219) | copy-start | bytes 3145732
  533.0 9.9 copy-start.10
  556.9 11.4 all-to-all-start.8
  561.9 245.0 %reduce-scatter.53.cloned.1.call-start = ((), (), s32[]{:S(2)}) async-start(), calls=%async_computation.51 | async-start | bytes 278528
  591.9 20.1 %all-to-all-start.11 = ((bf16[8,2,8192]{2,1,0:T(2,128)(2,1)}), bf16[8,2,8192]{2,1,0:T(2,128)(2,1)}, u32[]{:S(2)}, u32[]{:S(2)}) async-start(bf16[8,2,8192]{2,1,0:T(2,128)(2,1)} %reshape.619), calls=%async_computation.11 | async-start | bytes 524288 | tf_op jit(solution)/shard_map/all_to_all | solution.py:181
  612.0 13.1 all-to-all-start.10
  620.2 9.8 copy-start.23
  625.2 15.8 all-to-all-start.9
  630.0 188.8 %reduce-scatter.33.cloned.1.call-start = ((), (), s32[]{:S(2)}) async-start(), calls=%async_computation.33 | async-start | bytes 2228224 | tf_op jit(solution)/shard_map/reduce_scatter | solution.py:227
  633.0 185.8 %reduce-scatter.31.cloned.1.call-start = ((), (), s32[]{:S(2)}) async-start(), calls=%async_computation.32 | async-start | bytes 2228224 | tf_op jit(solution)/shard_map/reduce_scatter | solution.py:227
  636.1 10.4 copy-start.28
  641.0 10.9 copy-start.30
  646.5 16.6 slice-start
  670.2 206.0 %reduce-scatter.29.cloned.1.call-start = ((), (), s32[]{:S(2)}) async-start(), calls=%async_computation.31 | async-start | bytes 6684672 | tf_op jit(solution)/shard_map/reduce_scatter | solution.py:224
  686.5 11.3 all-to-all-start.12
  704.9 12.8 copy-start.43
  712.4 22.1 %all-to-all-start.15 = ((bf16[8,2,8192]{2,1,0:T(2,128)(2,1)}), bf16[8,2,8192]{2,1,0:T(2,128)(2,1)}, u32[]{:S(2)}, u32[]{:S(2)}) async-start(bf16[8,2,8192]{2,1,0:T(2,128)(2,1)} %reshape.627), calls=%async_computation.15 | async-start | bytes 524288 | tf_op jit(solution)/shard_map/all_to_all | solution.py:181
  734.5 12.9 all-to-all-start.14
  747.4 13.7 all-to-all-start.13
  752.3 208.5 %reduce-scatter.27.cloned.1.call-start = ((), (), s32[]{:S(2)}) async-start(), calls=%async_computation.30 | async-start | bytes 6684672 | tf_op jit(solution)/shard_map/reduce_scatter | solution.py:224
  755.4 11.1 copy-start.33
  755.4 11.1 copy-start.5
  755.4 11.1 copy-start.53
  755.4 11.1 copy-start.55
  755.4 11.1 copy-start.60
  755.4 11.1 copy-start.62
  772.2 276.4 %reduce-scatter.37.cloned.1.call-start = ((), (), s32[]{:S(2)}) async-start(), calls=%async_computation.35 | async-start | bytes 8912896 | tf_op jit(solution)/shard_map/reduce_scatter | solution.py:230
  779.4 357.3 %reduce-scatter.41.cloned.1.call-start = ((), (), s32[]{:S(2)}) async-start(), calls=%async_computation.37 | async-start | bytes 8912896 | tf_op jit(solution)/shard_map/reduce_scatter | solution.py:233
  785.1 439.6 %reduce-scatter.35.cloned.1.call-start = ((), (), s32[]{:S(2)}) async-start(), calls=%async_computation.34 | async-start | bytes 8912896 | tf_op jit(solution)/shard_map/reduce_scatter | solution.py:230
  792.0 520.6 %reduce-scatter.39.cloned.1.call-start = ((), (), s32[]{:S(2)}) async-start(), calls=%async_computation.36 | async-start | bytes 8912896 | tf_op jit(solution)/shard_map/reduce_scatter | solution.py:233
  798.8 588.0 %reduce-scatter.49.cloned.1.call-start = ((), (), s32[]{:S(2)}) async-start(), calls=%async_computation.49 | async-start | bytes 278528
  808.7 653.2 %reduce-scatter.45.cloned.1.call-start = ((), (), s32[]{:S(2)}) async-start(), calls=%async_computation.47 | async-start | bytes 278528
  809.7 726.8 %reduce-scatter.51.cloned.1.call-start = ((), (), s32[]{:S(2)}) async-start(), calls=%async_computation.50 | async-start | bytes 278528
  811.0 800.5 %reduce-scatter.43.cloned.1.call-start = ((), (), s32[]{:S(2)}) async-start(), calls=%async_computation.46 | async-start | bytes 278528
  817.7 868.6 %reduce-scatter.47.cloned.1.call-start = ((), (), s32[]{:S(2)}) async-start(), calls=%async_computation.48 | async-start | bytes 278528
  818.7 777.0 %copy-start.15 = (f32[128,1024]{1,0:T(8,128)S(1)}, f32[128,1024]{1,0:T(8,128)}, u32[]{:S(2)}) copy-start(f32[128,1024]{1,0:T(8,128)} %copy-done.14) | copy-start | bytes 1572868
  818.7 939.1 %all-reduce.9.cloned.1.call-start = ((), (), s32[]{:S(2)}) async-start(), calls=%async_computation.52 | async-start | bytes 6291456 | tf_op jit(solution)/shard_map/psum | solution.py:253
  (50 other events, 187.5 us)
Sparse Core Ops, SparseCore 0:
  10.7 66.7 all-gather.26
  79.7 43.8 all-gather.28
  126.3 73.3 all-gather.30
  202.3 73.1 all-gather.32
  277.5 60.9 all-gather.34
  340.5 43.8 all-gather.36
  387.1 73.5 all-gather.38
  462.8 70.1 all-gather.40
  565.9 69.9 reduce-scatter.52
  639.9 73.7 reduce-scatter.32
  717.5 73.6 reduce-scatter.30
  794.9 81.1 reduce-scatter.28
  880.0 80.8 reduce-scatter.26
  964.5 84.0 reduce-scatter.36
  1052.2 84.3 reduce-scatter.40
  1140.3 84.3 reduce-scatter.34
  1228.3 84.1 reduce-scatter.38
  1315.9 70.8 reduce-scatter.48
  1390.6 71.2 reduce-scatter.44
  1465.2 71.2 reduce-scatter.50
  1540.2 71.2 reduce-scatter.42
  1615.0 71.2 reduce-scatter.46
  1689.1 68.6 all-reduce.8
where the time goes:
time: 1780 us; the launch traced here: 1770 us
  waiting for transfers between devices  1020 us (57%)
  blocking collectives  262 us (15%)
  matrix products  162 us (9%)
  local copies, waits for them, and re-layouts  136 us (8%)
  starting transfers between devices  102 us (6%)
  other arithmetic  75.9 us (4%)
  between operations  17.9 us (1%)
    unnamed x29, waiting for transfers between devices  314 us
    reduce_scatter x2, waiting for transfers between devices, share_gradients(): lax.psum_scatter(grad_downw.astype(jnp.bfloat16), 'dp', scatter_dimension...  176 us
    reduce_scatter x2, waiting for transfers between devices, share_gradients(): lax.psum_scatter(grad_upw.astype(jnp.bfloat16), 'dp', scatter_dimension=0...  176 us
    reduce_scatter x2, waiting for transfers between devices, share_gradients(): lax.psum_scatter(grad_qkvw.astype(jnp.bfloat16), 'dp', scatter_dimension=...  142 us
    unnamed x220, local copies, waits for them, and re-layouts  65.2 us
    all_gather x2, waiting for transfers between devices, shards(): lax.all_gather(w_down[layer_index], 'dp', axis=0, tiled=True)  63.2 us
    unnamed x1, blocking collectives  57.9 us
    psum x1, waiting for transfers between devices, share_gradients(): lax.psum(owned[0].astype(jnp.bfloat16), 'seq').astype(jnp.float32)  53.6 us
  transfers between devices with their start and end apart: 39, of which 21 were waited for; matrix products, arithmetic and copies ran while one was open for 19% of the time, Pallas kernels for 0%

commit v1 on v0

v1 whole, which is shorter than its diff:
```python
import jax
import jax.numpy as jnp
from jax import lax
from jax.sharding import PartitionSpec as P

EPSILON = 1e-06
BF = jnp.bfloat16
F32 = jnp.float32
BLOCK = 80
SHARE = 73
TOTAL = 577

NEXT = [(i, (i + 2) % 8) for i in range(8)]
PREV = [(i, (i - 2) % 8) for i in range(8)]
FAR = [(i, (i + 4) % 8) for i in range(8)]
CORE = [(i, i ^ 1) for i in range(8)]


def x_gather(block):
    return [
        block,
        lax.ppermute(block, "seq", PREV),
        lax.ppermute(block, "seq", FAR),
        lax.ppermute(block, "seq", NEXT),
    ]


def x_scatter(blocks):
    return [
        blocks[0],
        lax.ppermute(blocks[1], "seq", NEXT),
        lax.ppermute(blocks[2], "seq", FAR),
        lax.ppermute(blocks[3], "seq", PREV),
    ]


def core_swap(v):
    return lax.ppermute(v, "seq", CORE)


def dot(a, b):
    return jnp.dot(a, b, preferred_element_type=F32)


def dot_nt(a, b):
    return lax.dot_general(a, b, (((1,), (1,)), ((), ())), preferred_element_type=F32)


def dot_tn(a, b):
    return lax.dot_general(a, b, (((0,), (0,)), ((), ())), preferred_element_type=F32)


def norm_parts(rows):
    mean = jnp.mean(rows, axis=-1, keepdims=True)
    centered = rows - mean
    rstd = lax.rsqrt(jnp.mean(centered * centered, axis=-1, keepdims=True) + EPSILON)
    return centered * rstd, rstd


def layer_norm(rows, gain, shift):
    return (norm_parts(rows)[0] * gain + shift).astype(BF)


def norm_back(rows, gain, err):
    n, rstd = norm_parts(rows)
    eg = err * gain
    back = rstd * (
        eg - jnp.mean(eg, axis=-1, keepdims=True) - n * jnp.mean(eg * n, axis=-1, keepdims=True)
    )
    return back, jnp.sum(err * n, axis=0), jnp.sum(err, axis=0)


def heads(v):
    return v.reshape(v.shape[0], 4, 64)


def attend(q, k, v, keep):
    s = jnp.einsum("qhd,khd->hqk", heads(q), heads(k), preferred_element_type=F32) * 0.125
    s = jnp.where(keep[None], s, -1e9)
    top = jnp.max(s, axis=-1, keepdims=True)
    e = jnp.exp(s - top)
    total = jnp.sum(e, axis=-1, keepdims=True)
    p = (e / total).astype(BF)
    mixed = jnp.einsum("hqk,khd->qhd", p, heads(v), preferred_element_type=F32)
    return mixed.reshape(q.shape).astype(BF), top + jnp.log(total)


def attend_back(q, k, v, keep, lse, dmixed):
    s = jnp.einsum("qhd,khd->hqk", heads(q), heads(k), preferred_element_type=F32) * 0.125
    s = jnp.where(keep[None], s, -1e9)
    p = jnp.exp(s - lse)
    dp = jnp.einsum("qhd,khd->hqk", heads(dmixed), heads(v), preferred_element_type=F32)
    inner = jnp.sum(dp * p, axis=-1, keepdims=True)
    ds = (p * (dp - inner)).astype(BF)
    dq = jnp.einsum("hqk,khd->qhd", ds, heads(k), preferred_element_type=F32) * 0.125
    dk = jnp.einsum("hqk,qhd->khd", ds, heads(q), preferred_element_type=F32) * 0.125
    dv = jnp.einsum("hqk,qhd->khd", p.astype(BF), heads(dmixed), preferred_element_type=F32)
    return dq.reshape(q.shape), dk.reshape(k.shape), dv.reshape(v.shape)


def swap_halves(v):
    n = v.shape[-1] // 2
    return jnp.concatenate([v[..., n:], v[..., :n]], axis=-1)


def shards(tokens, counts, cotangent, w_qkv, w_out, w_up, w_down, norm_gain, norm_shift,
           bias_qv, bias_up, bias_branch):
    s = lax.axis_index("seq")
    x = s // 2
    c = s % 2
    at = lambda v, i, axis: lax.dynamic_index_in_dim(v, i, axis, keepdims=False)

    live = counts[0]
    start = jnp.cumsum(live) - live
    slot = jnp.arange(1024, dtype=jnp.int32)
    in_slot = slot % 128
    slot_rank = jnp.where(in_slot < jnp.repeat(live, 128), jnp.repeat(start, 128) + in_slot, -1)

    def ranks(core):
        r = jnp.arange(4 * BLOCK, dtype=jnp.int32)
        within = r % BLOCK
        rank = (core * 4 + (x + r // BLOCK) % 4) * SHARE + within
        return jnp.where((within < SHARE) & (rank < TOTAL), rank, -2)

    mine_rank, other_rank = ranks(c), ranks(1 - c)
    keep = (jnp.concatenate([mine_rank, other_rank]) >= 0)[None, :]
    order = ((x + jnp.arange(4)) % 4 * 2)[None, :] + jnp.stack([c, 1 - c])[:, None]
    came_rank = slot_rank.reshape(8, 128)[order.reshape(8)].reshape(1024)
    pick = (mine_rank[:, None] == came_rank[None, :]).astype(BF)
    own_rank = at(slot_rank.reshape(8, 128), s, 0)
    place = (own_rank[:, None] == jnp.concatenate([mine_rank, other_rank])[None, :]).astype(BF)

    def compact(rows):
        half = jnp.concatenate(x_gather(rows), axis=0)
        return dot(pick, jnp.concatenate([half, core_swap(half)], axis=0)).astype(BF)

    def spread(block):
        half = jnp.concatenate(x_gather(block), axis=0)
        return dot(place, jnp.concatenate([half, core_swap(half)], axis=0)).astype(BF)

    def offered(l):
        qkv = at(w_qkv[l].reshape(64, 3, 8, 128), 2 * x + c, 2).reshape(64, 384)
        up = at(at(w_up[l].reshape(64, 2, 8, 4, 64), c, 1), x, 2).reshape(64, 512)
        out = at(w_out[l].reshape(64, 2, 512), c, 1)
        down = at(at(w_down[l].reshape(4, 64, 2, 512), x, 0), c, 1)
        return jnp.concatenate([qkv, up, out, down], axis=1)

    small = jnp.concatenate([norm_gain.reshape(-1), norm_shift.reshape(-1), bias_branch.reshape(-1),
                             bias_qv.reshape(-1), bias_up.reshape(-1)])
    small = lax.all_gather(small.reshape(12, 128), "dp", axis=0).reshape(16, 1536).astype(F32)
    per_d = lambda i: small[:, i:i + 256].reshape(16, 2, 2, 64).transpose(1, 2, 0, 3).reshape(2, 2, 1024)
    gains, shifts, branch = per_d(0), per_d(256), per_d(512)
    qv = small[:, 768:1024].reshape(2, 8, 2, 128)
    upb = small[:, 1024:1536].reshape(2, 8, 2, 4, 64)

    weights = []
    for l in range(2):
        mine = lax.all_gather(offered(l), "dp", axis=0, tiled=True)
        other = core_swap(mine)
        w = []
        for v, cc in ((mine, c), (other, 1 - c)):
            qb, vb = at(qv[0, :, l], 2 * x + cc, 0), at(qv[1, :, l], 2 * x + cc, 0)
            w.append(dict(qkv=v[:, :384], up=v[:, 384:896], out=v[:, 896:1408], down=v[:, 1408:],
                          qkv_bias=jnp.concatenate([qb, jnp.zeros((128,), F32), vb]),
                          up_bias=at(at(upb[:, :, l], cc, 0), x, 1).reshape(512)))
        full_out = jnp.where(c == 0, jnp.concatenate([w[0]["out"], w[1]["out"]], 1),
                             jnp.concatenate([w[1]["out"], w[0]["out"]], 1))
        pairs = jnp.stack([2 * ((x + j) % 4) + (c + i) % 2 for j in range(4) for i in range(2)])
        full_out = full_out.reshape(8, 128, 1024)[pairs].reshape(1024, 1024)
        down = [jnp.concatenate([at(v["down"].reshape(2, 512, 512), cc, 0) for cc in (c, 1 - c)], 0) for v in w]
        down = jnp.where(c == 0, jnp.concatenate(down, 1), jnp.concatenate(down[::-1], 1))
        weights.append(dict(
            qkv=jnp.concatenate([w[0]["qkv"], w[1]["qkv"]], 1),
            qkv_bias=jnp.concatenate([w[0]["qkv_bias"], w[1]["qkv_bias"]]),
            up=jnp.concatenate([w[0]["up"], w[1]["up"]], 1),
            up_bias=jnp.concatenate([w[0]["up_bias"], w[1]["up_bias"]]),
            out=full_out, down=down))

    hidden = compact(tokens[0]).astype(F32)
    kept = []
    for l in range(2):
        w = weights[l]
        a = layer_norm(hidden, gains[l, 0], shifts[l, 0])
        packed = (dot(a, w["qkv"]) + w["qkv_bias"]).astype(BF)
        q = jnp.concatenate([packed[:, :128], packed[:, 384:512]], 1)
        k = jnp.concatenate([packed[:, 128:256], packed[:, 512:640]], 1)
        v = jnp.concatenate([packed[:, 256:384], packed[:, 640:]], 1)
        far = core_swap(jnp.concatenate([swap_halves(k), swap_halves(v)], 1))
        k = jnp.concatenate([k, far[:, :256]], 0)
        v = jnp.concatenate([v, far[:, 256:]], 0)
        mixed, lse = attend(q, k, v, keep)
        came = x_gather(mixed)
        came = [jnp.roll(m.reshape(4, BLOCK, 256), j, axis=0).reshape(4 * BLOCK, 256) for j, m in enumerate(came)]
        all_mixed = jnp.concatenate(came, axis=1)
        middle = hidden + dot(all_mixed, w["out"]) + branch[l, 0]
        cc = layer_norm(middle, gains[l, 1], shifts[l, 1])
        u = dot(cc, w["up"]) + w["up_bias"]
        g, gelu_back = jax.vjp(lambda t: jax.nn.gelu(t, approximate=False), u)
        g = g.astype(BF)
        slope = gelu_back(jnp.ones_like(u))[0]
        part = dot(g, w["down"]).astype(BF).reshape(4, BLOCK, 1024)
        mlp = sum(t.astype(F32) for t in x_scatter([part[j] for j in range(4)]))
        kept.append((hidden, a, q, k, v, lse, all_mixed, middle, cc, g, slope))
        if l == 0:
            mlp = jnp.concatenate(x_gather(mlp.astype(BF)), axis=0).astype(F32)
            hidden = middle + mlp + branch[l, 1]
        else:
            last = middle[:BLOCK] + mlp + branch[l, 1]
    output = spread(last.astype(BF))

    dz = compact(cotangent[0])
    dh = dz[:BLOCK].astype(F32)
    big, tiny = [None, None], [None, None]
    for l in (1, 0):
        w = weights[l]
        hidden, a, q, k, v, lse, all_mixed, middle, cc, g, slope = kept[l]
        du = (dot_nt(dz, w["down"]) * slope).astype(BF)
        part = dot_nt(du, w["up"]).astype(BF).reshape(4, BLOCK, 1024)
        err = sum(t.astype(F32) for t in x_scatter([part[j] for j in range(4)]))
        d_down = dot_tn(g, dz)
        d_up = dot_tn(cc, du)
        d_up_bias = jnp.sum(du.astype(F32), axis=0)
        d_branch1 = jnp.sum(dz[:BLOCK].astype(F32), axis=0)
        back, d_gain1, d_shift1 = norm_back(middle[:BLOCK], gains[l, 1], err)
        dm = dh + back
        dmb = dm.astype(BF)
        d_branch0 = jnp.sum(dmb.astype(F32), axis=0)
        dmb = jnp.concatenate(x_gather(dmb), axis=0)
        dmixed = dot_nt(dmb, w["out"][:256]).astype(BF)
        dq, dk, dv = attend_back(q, k, v, keep, lse, dmixed)
        n = 4 * BLOCK
        far = core_swap(jnp.concatenate([swap_halves(dk[n:]), swap_halves(dv[n:])], 1).astype(BF)).astype(F32)
        dq = dq.astype(BF)
        dk = (dk[:n] + far[:, :256]).astype(BF)
        dv = (dv[:n] + far[:, 256:]).astype(BF)
        dpacked = jnp.concatenate([dq[:, :128], dk[:, :128], dv[:, :128], dq[:, 128:], dk[:, 128:], dv[:, 128:]], 1)
        part = dot_nt(dpacked, w["qkv"]).astype(BF).reshape(4, BLOCK, 1024)
        err = sum(t.astype(F32) for t in x_scatter([part[j] for j in range(4)]))
        d_qkv = dot_tn(a, dpacked)
        d_qv = jnp.sum(dpacked.astype(F32), axis=0)
        d_out = dot_tn(all_mixed, lax.dynamic_slice_in_dim(dmb, 256 * x, 256, 1))
        back, d_gain0, d_shift0 = norm_back(hidden[:BLOCK], gains[l, 0], err)
        dh = dm + back
        dz = dh.astype(BF)
        if l == 1:
            dz = jnp.concatenate(x_gather(dz), axis=0)

        pair_at = [((2 * ((p // 2 - x) % 4)) + (p % 2 - c) % 2) for p in range(8)]
        d_out = d_out.reshape(8, 128, 256)[jnp.stack(pair_at)].reshape(1024, 256)
        halves = []
        for i, core in ((0, c), (1, 1 - c)):
            dd = lax.dynamic_slice_in_dim(d_down, core * 512, 512, 1).reshape(2, 512, 512)
            dd = jnp.concatenate([at(dd, c, 0), at(dd, 1 - c, 0)], 0)
            halves.append(jnp.concatenate([
                d_qkv[:, 384 * i:384 * (i + 1)], d_up[:, 512 * i:512 * (i + 1)],
                lax.dynamic_slice_in_dim(d_out, 128 * core, 128, 1), dd], axis=1).astype(BF))
        grads = (halves[0].astype(F32) + core_swap(halves[1]).astype(F32)).astype(BF)
        got = lax.all_to_all(grads.reshape(16, 64, 1536), "dp", split_axis=0, concat_axis=0, tiled=True)
        got = jnp.sum(got.astype(F32), axis=0).astype(BF)
        half = jnp.stack(x_gather(got))
        both = jnp.stack([half, core_swap(half)])
        both = jnp.stack([at(both, c, 0), at(both, 1 - c, 0)], 1)
        both = jnp.stack([at(both, (j - x) % 4, 0) for j in range(4)])
        big[l] = (
            both[..., :384].reshape(4, 2, 64, 3, 128).transpose(2, 3, 0, 1, 4).reshape(64, 3072),
            both[..., 896:1024].transpose(2, 0, 1, 3).reshape(64, 1024),
            both[..., 384:896].reshape(4, 2, 64, 8, 64).transpose(2, 1, 3, 0, 4).reshape(64, 4096),
            both[..., 1024:].transpose(0, 2, 1, 3).reshape(256, 1024),
        )
        tiny[l] = (jnp.stack([d_gain0, d_gain1]), jnp.stack([d_shift0, d_shift1]),
                   jnp.stack([d_branch0, d_branch1]), d_qv, d_up_bias)
    grad_tokens = spread(dz)

    pieces = []
    by_d = lambda member: jnp.stack([tiny[0][member], tiny[1][member]]).reshape(4, 16, 64).transpose(1, 0, 2).reshape(16, 256)
    pair = jnp.arange(8)
    qv_all = jnp.zeros((2, 2, 8, 128), F32)
    up_all = jnp.zeros((2, 2, 8, 4, 64), F32)
    for l in range(2):
        d_qv, d_up_bias = tiny[l][3], tiny[l][4]
        for i, core in ((0, c), (1, 1 - c)):
            here = (pair == 2 * x + core)[:, None]
            qv_all = qv_all.at[l, 0].add(jnp.where(here, d_qv[384 * i:384 * i + 128], 0.0))
            qv_all = qv_all.at[l, 1].add(jnp.where(here, d_qv[384 * i + 256:384 * i + 384], 0.0))
            here = (jnp.arange(2) == core)[:, None, None, None] & (jnp.arange(4) == x)[None, None, :, None]
            up_all = up_all.at[l].add(jnp.where(here, d_up_bias[512 * i:512 * (i + 1)].reshape(1, 8, 1, 64), 0.0))
    pieces = [by_d(0), by_d(1), by_d(2),
              qv_all.reshape(2, 16, 128).transpose(1, 0, 2).reshape(16, 256),
              up_all.reshape(2, 16, 256).transpose(1, 0, 2).reshape(16, 512)]
    tiny_all = jnp.concatenate(pieces, 1).reshape(16, 12, 128)
    got = lax.all_to_all(tiny_all, "dp", split_axis=0, concat_axis=0, tiled=True)
    got = jnp.sum(got, axis=0)
    got = sum(x_gather(got))
    got = (got + core_swap(got)).reshape(-1)
    lead = lambda i: jnp.stack([big[0][i], big[1][i]]).astype(F32)
    return (
        output[None], spread_shape(grad_tokens),
        lead(0), lead(1), lead(2), lead(3),
        got[:256].reshape(2, 2, 64), got[256:512].reshape(2, 2, 64),
        got[768:1024].reshape(2, 128), got[1024:].reshape(2, 256),
        got[512:768].reshape(2, 2, 64),
    )


def spread_shape(v):
    return v[None]


def solution(mesh):
    rows = P("dp", "seq", None)
    mid = P(None, "dp", None)
    end = P(None, None, "dp")
    two = P(None, "dp")
    return jax.shard_map(
        shards,
        mesh=mesh,
        in_specs=(rows, P("dp", None), rows, mid, mid, mid, mid, end, end, two, two, end),
        out_specs=(rows, rows, mid, mid, mid, mid, end, end, two, two, end),
        check_vma=False,
    )
```

time: 1780 us -> 620 us (0.35)
  waiting for transfers between devices: 1020 us -> 117 us
  blocking collectives: 262 us -> 20.9 us
  matrix products: 162 us -> 69.2 us
  local copies, waits for them, and re-layouts: 136 us -> 171 us
  other arithmetic: 75.9 us -> 98.8 us
    reduce_scatter x8 -> x0, waiting for transfers between devices: 494 us -> none  [the longest x2 176 us: share_gradients(): lax.psum_scatter(grad_downw.astype(jnp.bfloat16), 'dp', scatter_dimension...]
    unnamed x29 -> x2, waiting for transfers between devices: 314 us -> 0.03 us
    all_gather x10 -> x1, blocking collectives: 189 us -> 20.9 us  [shards(): lax.all_gather(small.reshape(12, 128), 'dp', axis=0).reshape(16, 1536)]
    ppermute x0 -> x72, starting transfers between devices: none -> 98 us  [the longest x13 28.2 us: x_gather(): lax.ppermute(block, 'seq', FAR)]
    dot_general x36 -> x40, matrix products: 162 us -> 69.2 us  [the longest x12 27.8 us: dot(): return jnp.dot(a, b, preferred_element_type=F32)]
    all_to_all x16 -> x3, starting transfers between devices: 100 us -> 15.9 us  [the longest x2 11.1 us: shards(): lax.all_to_all(grads.reshape(16, 64, 1536), 'dp', split_axis=0, concat_ax...]
    all_gather x8 -> x2, waiting for transfers between devices: 128 us -> 51.1 us  [shards(): mine = lax.all_gather(offered(l), 'dp', axis=0, tiled=True)]
    ppermute x0 -> x72, waiting for transfers between devices: none -> 57.9 us  [the longest x13 25.7 us: x_gather(): lax.ppermute(block, 'seq', FAR)]
  transfers between devices with their start and end apart: 39 -> 77, of which waited for: 21 -> 27; matrix products, arithmetic and copies ran while one was open for 19% -> 37% of each run, Pallas kernels for 0% -> 0%
where the time goes in v1:
time: 620 us; the launch traced here: 609 us
  local copies, waits for them, and re-layouts  171 us (28%)
  waiting for transfers between devices  117 us (19%)
  starting transfers between devices  114 us (18%)
  other arithmetic  98.8 us (16%)
  matrix products  69.2 us (11%)
  blocking collectives  20.9 us (3%)
  between operations  17.7 us (3%)
    unnamed x432, local copies, waits for them, and re-layouts  51.9 us
    all_gather x2, waiting for transfers between devices, shards(): mine = lax.all_gather(offered(l), 'dp', axis=0, tiled=True)  51.1 us
    ppermute x13, starting transfers between devices, x_gather(): lax.ppermute(block, 'seq', FAR)  28.2 us
    dot_general x12, matrix products, dot(): return jnp.dot(a, b, preferred_element_type=F32)  27.8 us
    ppermute x13, waiting for transfers between devices, x_gather(): lax.ppermute(block, 'seq', FAR)  25.7 us
    ppermute x15, starting transfers between devices, core_swap(): return lax.ppermute(v, 'seq', CORE)  24.8 us
    concatenate x2, other arithmetic, shards(): jnp.concatenate([d_qkv[:, 384 * i:384 * (i + 1)], d_up[:, 512 * i:512 * (...  21 us
    all_gather x1, blocking collectives, shards(): lax.all_gather(small.reshape(12, 128), 'dp', axis=0).reshape(16, 1536)  20.9 us
  transfers between devices with their start and end apart: 77, of which 27 were waited for; matrix products, arithmetic and copies ran while one was open for 37% of the time, Pallas kernels for 0%

profile of v1, /device:TPU:1, one launch (start us, length us, event | category | flops | bytes accessed | tf_op | source)
XLA Modules:
  0.0 608.9 jit_solution(12056313374187021962)
XLA Ops:
  20.3 2.1 collective-permute-start.2
  22.4 2.5 collective-permute-start.1
  28.8 20.9 %all_gather.9 = bf16[16,12,128]{2,1,0:T(8,128)(2,1)S(1)} all-gather(bf16[1,12,128]{2,1,0:T(8,128)(2,1)S(1)} %bitcast.562), channel_id=1, replica_groups=mesh['dp'=16,'seq'=8] {'dp'}, dimensions={0}, use_global_device_ids=true | all-gather | bytes 52224 | tf_op jit(solution)/shard_map/all_gather | solution.py:150
  60.2 7.1 %collective-permute-start.3 = (bf16[512,1024]{1,0:T(8,128)(2,1)S(1)}, bf16[512,1024]{1,0:T(8,128)(2,1)S(1)}, u32[]{:S(2)}, u32[]{:S(2)}) collective-permute-start(bf16[512,1024]{1,0:T(8,128)(2,1)S(1)} %pad_maximum_fusion.14), channel_id=1, source_target_pairs={{0,1},{1,0},{2,3},{3,2},{4,5},{5,4},{6,7},{7,6},{8,9},{9,8},{10,11... | collective-permute-start | bytes 3145736 | tf_op jit(solution)/shard_map/ppermute | solution.py:38
  67.3 2.8 all-gather.5.cloned.1.call-done
  74.4 48.4 %all-gather.3.cloned.1.call-done = bf16[1024,1920]{1,0:T(8,128)(2,1)} async-done(((bf16[64,1920]{1,0:T(8,128)(2,1)}), bf16[1024,1920]{1,0:T(8,128)(2,1)}) %all-gather.3.cloned.1.call-update) | async-done | bytes 3932176 | tf_op jit(solution)/shard_map/all_gather | solution.py:158
  129.3 2.7 fusion.194
  142.5 3.4 fusion.156
  150.4 3.6 fusion.158
  161.3 2.1 slice.1281
  176.2 2.4 collective-permute-start.7
  181.9 4.4 collective-permute-done.7
  186.5 2.7 fusion.196
  190.9 5.0 multiply_convert_fusion.3
  203.6 3.8 collective-permute-done.10
  208.1 2.7 collective-permute-start.13
  212.9 3.4 collective-permute-done.13
  223.9 2.9 collective-permute-start.16
  243.3 2.7 collective-permute-start.18
  246.0 3.7 collective-permute-done.19
  249.7 4.4 collective-permute-done.18
  254.9 2.7 fusion.198
  259.3 3.6 multiply_convert_fusion.2
  274.9 3.2 collective-permute-done.32
  283.5 2.1 copy.228
  285.6 2.1 copy.225
  287.7 2.1 copy.226
  289.8 2.1 copy.229
  292.5 2.4 convolution_convert_fusion.11
  296.6 2.9 fusion.47
  305.3 2.2 collective-permute-start.37
  310.0 2.5 gather_fusion.4
  328.9 10.5 %maximum_maximum_fusion.1 = bf16[1024,1536]{0,1:T(8,128)(2,1)} fusion(bf16[512,512]{0,1:T(8,128)(2,1)S(1)} %bitcast.439, bf16[512,512]{0,1:T(8,128)(2,1)S(1)} %bitcast.438, bf16[1024,128]{0,1:T(8,128)(2,1)S(1)} %copy-done.50, bf16[1024,512]{0,1:T(8,128)(2,1)S(1)} %copy-done.20, bf16[1024,384]{0,1:T(8,128)(2,1)S(1)} %get-tuple-element.237), kind=kLoop, calls=%fused_computation.20 | loop fusion | flops 15728640 | bytes 6291456 | tf_op jit(solution)/shard_map/concatenate | solution.py:254
  342.1 3.1 collective-permute-start.42
  349.2 3.9 collective-permute-done.42
  356.6 2.8 convolution_convert_fusion.1
  368.8 2.5 fusion.98
  373.6 2.1 copy.222
  377.8 3.1 fusion.159
  389.6 3.6 collective-permute-done.48
  393.4 2.4 convolution_convert_fusion.10
  407.2 2.7 collective-permute-start.50
  417.7 2.2 convolution_convert_fusion.4
  427.6 10.4 %maximum_maximum_fusion = bf16[1024,1536]{0,1:T(8,128)(2,1)} fusion(bf16[512,512]{0,1:T(8,128)(2,1)S(1)} %bitcast.437, bf16[512,512]{0,1:T(8,128)(2,1)S(1)} %bitcast.436, bf16[1024,128]{0,1:T(8,128)(2,1)S(1)} %copy.221, bf16[1024,512]{0,1:T(8,128)(2,1)S(1)} %copy-done.19, bf16[1024,384]{0,1:T(8,128)(2,1)S(1)} %get-tuple-element.229), kind=kLoop, calls=%fused_computation.19 | loop fusion | flops 15728640 | bytes 6291456 | tf_op jit(solution)/shard_map/concatenate | solution.py:254
  439.2 2.5 multiply_reduce_fusion.9
  442.9 4.8 all-to-all-start.2
  447.7 4.2 add_convert_fusion
  451.9 3.0 copy.184
  455.6 6.7 %all-to-all-start.1 = ((bf16[16,64,1536]{2,1,0:T(8,128)(2,1)}), bf16[16,64,1536]{2,1,0:T(8,128)(2,1)S(1)}, u32[]{:S(2)}, u32[]{:S(2)}) async-start(bf16[16,64,1536]{2,1,0:T(8,128)(2,1)} %bitcast.413), calls=%async_computation.1 | async-start | bytes 6291456 | tf_op jit(solution)/shard_map/all_to_all | solution.py:258
  462.3 3.3 convolution_convert_fusion.6
  473.4 4.1 collective-permute-done.21
  479.8 2.4 collective-permute-start.24
  484.0 2.1 copy.219
  489.0 7.1 %add_convert_fusion.1 = bf16[1024,1536]{0,1:T(8,128)(2,1)} fusion(bf16[1024,1536]{0,1:T(8,128)(2,1)} %collective-permute-done.58, bf16[512,512]{0,1:T(8,128)(2,1)} %bitcast.441, bf16[512,512]{0,1:T(8,128)(2,1)} %bitcast.440, bf16[1024,128]{0,1:T(8,128)(2,1)} %copy.218, bf16[1024,512]{0,1:T(8,128)(2,1)} %get-tuple-element.210, ...), kind=kLoop, calls=%fused_computation.6 | loop fusion | flops 20447232 | bytes 9437184 | tf_op jit(solution)/shard_map/convert_element_type | solution.py:257
  496.1 4.7 copy.176
  500.8 8.3 %all-to-all-done.1 = bf16[16,64,1536]{2,1,0:T(8,128)(2,1)S(1)} async-done(((bf16[16,64,1536]{2,1,0:T(8,128)(2,1)}), bf16[16,64,1536]{2,1,0:T(8,128)(2,1)S(1)}, u32[]{:S(2)}, u32[]{:S(2)}) %all-to-all-start.1) | async-done | bytes 3145760 | tf_op jit(solution)/shard_map/all_to_all | solution.py:258
  509.1 4.5 all-to-all-start
  513.6 2.1 pad_maximum_fusion.24
  540.5 2.4 fusion.59
  548.7 4.0 collective-permute-done.64
  562.1 2.3 reduce_sum.457
  564.5 3.2 collective-permute-start.60
  569.4 2.8 collective-permute-done.61
  572.2 4.7 collective-permute-done.60
  (916 shorter events, 301.3 us)
Async XLA Ops:
  7.2 62.9 %all-gather.5.cloned.1.call-start = ((), (), s32[]{:S(2)}) async-start(), calls=%async_computation.4 | async-start | bytes 4177920 | tf_op jit(solution)/shard_map/all_gather | solution.py:158
  16.1 106.7 %all-gather.3.cloned.1.call-start = ((), (), s32[]{:S(2)}) async-start(), calls=%async_computation.3 | async-start | bytes 4177920 | tf_op jit(solution)/shard_map/all_gather | solution.py:158
  20.3 38.1 %collective-permute-start.2 = (bf16[128,1024]{1,0:T(8,128)(2,1)S(1)}, bf16[128,1024]{1,0:T(8,128)(2,1)S(1)}, u32[]{:S(2)}, u32[]{:S(2)}) collective-permute-start(bf16[128,1024]{1,0:T(8,128)(2,1)S(1)} %bitcast.458), channel_id=1, source_target_pairs={{0,2},{1,3},{2,4},{3,5},{4,6},{5,7},{6,0},{7,1},{8,10},{9,11},{10,... | collective-permute-start | bytes 786440 | tf_op jit(solution)/shard_map/ppermute | solution.py:24
  22.4 37.0 %collective-permute-start.1 = (bf16[128,1024]{1,0:T(8,128)(2,1)S(1)}, bf16[128,1024]{1,0:T(8,128)(2,1)S(1)}, u32[]{:S(2)}, u32[]{:S(2)}) collective-permute-start(bf16[128,1024]{1,0:T(8,128)(2,1)S(1)} %bitcast.459), channel_id=1, source_target_pairs={{0,4},{1,5},{2,6},{3,7},{4,0},{5,1},{6,2},{7,3},{8,12},{9,13},{10,... | collective-permute-start | bytes 786440 | tf_op jit(solution)/shard_map/ppermute | solution.py:23
  24.8 34.6 %collective-permute-start = (bf16[128,1024]{1,0:T(8,128)(2,1)S(1)}, bf16[128,1024]{1,0:T(8,128)(2,1)S(1)}, u32[]{:S(2)}, u32[]{:S(2)}) collective-permute-start(bf16[128,1024]{1,0:T(8,128)(2,1)S(1)} %bitcast.460), channel_id=1, source_target_pairs={{0,6},{1,7},{2,0},{3,1},{4,2},{5,3},{6,4},{7,5},{8,14},{9,15},{10,... | collective-permute-start | bytes 786440 | tf_op jit(solution)/shard_map/ppermute | solution.py:22
  26.0 45.7 %collective-permute-start.29 = (bf16[128,1024]{1,0:T(8,128)(2,1)S(1)}, bf16[128,1024]{1,0:T(8,128)(2,1)S(1)}, u32[]{:S(2)}, u32[]{:S(2)}) collective-permute-start(bf16[128,1024]{1,0:T(8,128)(2,1)S(1)} %bitcast.462), channel_id=1, source_target_pairs={{0,2},{1,3},{2,4},{3,5},{4,6},{5,7},{6,0},{7,1},{8,10},{9,11},{10,... | collective-permute-start | bytes 786440 | tf_op jit(solution)/shard_map/ppermute | solution.py:24
  26.3 45.4 %collective-permute-start.28 = (bf16[128,1024]{1,0:T(8,128)(2,1)S(1)}, bf16[128,1024]{1,0:T(8,128)(2,1)S(1)}, u32[]{:S(2)}, u32[]{:S(2)}) collective-permute-start(bf16[128,1024]{1,0:T(8,128)(2,1)S(1)} %bitcast.463), channel_id=1, source_target_pairs={{0,4},{1,5},{2,6},{3,7},{4,0},{5,1},{6,2},{7,3},{8,12},{9,13},{10,... | collective-permute-start | bytes 786440 | tf_op jit(solution)/shard_map/ppermute | solution.py:23
  58.4 13.3 %collective-permute-start.27 = (bf16[128,1024]{1,0:T(8,128)(2,1)S(1)}, bf16[128,1024]{1,0:T(8,128)(2,1)}, u32[]{:S(2)}, u32[]{:S(2)}) collective-permute-start(bf16[128,1024]{1,0:T(8,128)(2,1)S(1)} %bitcast.464), channel_id=1, source_target_pairs={{0,6},{1,7},{2,0},{3,1},{4,2},{5,3},{6,4},{7,5},{8,14},{9,15},{10,... | collective-permute-start | bytes 786440 | tf_op jit(solution)/shard_map/ppermute | solution.py:22
  60.2 68.1 %collective-permute-start.3 = (bf16[512,1024]{1,0:T(8,128)(2,1)S(1)}, bf16[512,1024]{1,0:T(8,128)(2,1)S(1)}, u32[]{:S(2)}, u32[]{:S(2)}) collective-permute-start(bf16[512,1024]{1,0:T(8,128)(2,1)S(1)} %pad_maximum_fusion.14), channel_id=1, source_target_pairs={{0,1},{1,0},{2,3},{3,2},{4,5},{5,4},{6,7},{7,6},{8,9},{9,8},{10,11... | collective-permute-start | bytes 3145736 | tf_op jit(solution)/shard_map/ppermute | solution.py:38
  70.1 72.4 %collective-permute-start.15 = (bf16[1024,1920]{1,0:T(8,128)(2,1)}, bf16[1024,1920]{1,0:T(8,128)(2,1)}, u32[]{:S(2)}, u32[]{:S(2)}) collective-permute-start(bf16[1024,1920]{1,0:T(8,128)(2,1)} %all-gather.5.cloned.1.call-done), channel_id=1, source_target_pairs={{0,1},{1,0},{2,3},{3,2},{4,5},{5,4},{6,7},{7,6},{8,9},{9,8},{10,11... | collective-permute-start | bytes 11796488 | tf_op jit(solution)/shard_map/ppermute | solution.py:38
  73.7 58.7 %collective-permute-start.30 = (bf16[512,1024]{1,0:T(8,128)(2,1)}, bf16[512,1024]{1,0:T(8,128)(2,1)}, u32[]{:S(2)}, u32[]{:S(2)}) collective-permute-start(bf16[512,1024]{1,0:T(8,128)(2,1)} %pad_maximum_fusion.15), channel_id=1, source_target_pairs={{0,1},{1,0},{2,3},{3,2},{4,5},{5,4},{6,7},{7,6},{8,9},{9,8},{10,11... | collective-permute-start | bytes 3145736 | tf_op jit(solution)/shard_map/ppermute | solution.py:38
  122.8 27.6 %collective-permute-start.4 = (bf16[1024,1920]{1,0:T(8,128)(2,1)}, bf16[1024,1920]{1,0:T(8,128)(2,1)}, u32[]{:S(2)}, u32[]{:S(2)}) collective-permute-start(bf16[1024,1920]{1,0:T(8,128)(2,1)} %all-gather.3.cloned.1.call-done), channel_id=1, source_target_pairs={{0,1},{1,0},{2,3},{3,2},{4,5},{5,4},{6,7},{7,6},{8,9},{9,8},{10,11... | collective-permute-start | bytes 11796488 | tf_op jit(solution)/shard_map/ppermute | solution.py:38
  159.2 7.9 %collective-permute-start.5 = (bf16[320,512]{1,0:T(8,128)(2,1)S(1)}, bf16[320,512]{1,0:T(8,128)(2,1)S(1)}, u32[]{:S(2)}, u32[]{:S(2)}) collective-permute-start(bf16[320,512]{1,0:T(8,128)(2,1)S(1)} %pad_maximum_fusion.31), channel_id=1, source_target_pairs={{0,1},{1,0},{2,3},{3,2},{4,5},{5,4},{6,7},{7,6},{8,9},{9,8},{10,11... | collective-permute-start | bytes 983048 | tf_op jit(solution)/shard_map/ppermute | solution.py:38
  175.0 6.8 %collective-permute-start.8 = (bf16[320,256]{1,0:T(8,128)(2,1)}, bf16[320,256]{1,0:T(8,128)(2,1)S(1)}, u32[]{:S(2)}, u32[]{:S(2)}) collective-permute-start(bf16[320,256]{1,0:T(8,128)(2,1)} %copy.156), channel_id=1, source_target_pairs={{0,2},{1,3},{2,4},{3,5},{4,6},{5,7},{6,0},{7,1},{8,10},{9,11},{10,... | collective-permute-start | bytes 491528 | tf_op jit(solution)/shard_map/ppermute | solution.py:24
  176.2 10.1 %collective-permute-start.7 = (bf16[320,256]{1,0:T(8,128)(2,1)}, bf16[320,256]{1,0:T(8,128)(2,1)S(1)}, u32[]{:S(2)}, u32[]{:S(2)}) collective-permute-start(bf16[320,256]{1,0:T(8,128)(2,1)} %copy.156), channel_id=1, source_target_pairs={{0,4},{1,5},{2,6},{3,7},{4,0},{5,1},{6,2},{7,3},{8,12},{9,13},{10,... | collective-permute-start | bytes 491528 | tf_op jit(solution)/shard_map/ppermute | solution.py:23
  178.6 7.8 %collective-permute-start.6 = (bf16[320,256]{1,0:T(8,128)(2,1)}, bf16[320,256]{1,0:T(8,128)(2,1)S(1)}, u32[]{:S(2)}, u32[]{:S(2)}) collective-permute-start(bf16[320,256]{1,0:T(8,128)(2,1)} %copy.156), channel_id=1, source_target_pairs={{0,6},{1,7},{2,0},{3,1},{4,2},{5,3},{6,4},{7,5},{8,14},{9,15},{10,... | collective-permute-start | bytes 491528 | tf_op jit(solution)/shard_map/ppermute | solution.py:22
  199.7 7.7 %collective-permute-start.10 = (bf16[80,1024]{1,0:T(8,128)(2,1)S(1)}, bf16[80,1024]{1,0:T(8,128)(2,1)S(1)}, u32[]{:S(2)}, u32[]{:S(2)}) collective-permute-start(bf16[80,1024]{1,0:T(8,128)(2,1)S(1)} %get-tuple-element.286), channel_id=1, source_target_pairs={{0,4},{1,5},{2,6},{3,7},{4,0},{5,1},{6,2},{7,3},{8,12},{9,13},{10,... | collective-permute-start | bytes 491528 | tf_op jit(solution)/shard_map/ppermute | solution.py:32
  208.1 8.2 %collective-permute-start.13 = (bf16[80,1024]{1,0:T(8,128)(2,1)S(1)}, bf16[80,1024]{1,0:T(8,128)(2,1)S(1)}, u32[]{:S(2)}, u32[]{:S(2)}) collective-permute-start(bf16[80,1024]{1,0:T(8,128)(2,1)S(1)} %add_convert_fusion.8), channel_id=1, source_target_pairs={{0,4},{1,5},{2,6},{3,7},{4,0},{5,1},{6,2},{7,3},{8,12},{9,13},{10,... | collective-permute-start | bytes 491528 | tf_op jit(solution)/shard_map/ppermute | solution.py:23
  242.4 7.2 %collective-permute-start.19 = (bf16[320,256]{1,0:T(8,128)(2,1)}, bf16[320,256]{1,0:T(8,128)(2,1)S(1)}, u32[]{:S(2)}, u32[]{:S(2)}) collective-permute-start(bf16[320,256]{1,0:T(8,128)(2,1)} %copy.168), channel_id=1, source_target_pairs={{0,2},{1,3},{2,4},{3,5},{4,6},{5,7},{6,0},{7,1},{8,10},{9,11},{10,... | collective-permute-start | bytes 491528 | tf_op jit(solution)/shard_map/ppermute | solution.py:24
  243.3 10.8 %collective-permute-start.18 = (bf16[320,256]{1,0:T(8,128)(2,1)}, bf16[320,256]{1,0:T(8,128)(2,1)S(1)}, u32[]{:S(2)}, u32[]{:S(2)}) collective-permute-start(bf16[320,256]{1,0:T(8,128)(2,1)} %copy.168), channel_id=1, source_target_pairs={{0,4},{1,5},{2,6},{3,7},{4,0},{5,1},{6,2},{7,3},{8,12},{9,13},{10,... | collective-permute-start | bytes 491528 | tf_op jit(solution)/shard_map/ppermute | solution.py:23
  246.0 8.2 %collective-permute-start.17 = (bf16[320,256]{1,0:T(8,128)(2,1)}, bf16[320,256]{1,0:T(8,128)(2,1)S(1)}, u32[]{:S(2)}, u32[]{:S(2)}) collective-permute-start(bf16[320,256]{1,0:T(8,128)(2,1)} %copy.168), channel_id=1, source_target_pairs={{0,6},{1,7},{2,0},{3,1},{4,2},{5,3},{6,4},{7,5},{8,14},{9,15},{10,... | collective-permute-start | bytes 491528 | tf_op jit(solution)/shard_map/ppermute | solution.py:22
  266.8 8.1 %collective-permute-start.31 = (bf16[80,1024]{1,0:T(8,128)(2,1)S(1)}, bf16[80,1024]{1,0:T(8,128)(2,1)S(1)}, u32[]{:S(2)}, u32[]{:S(2)}) collective-permute-start(bf16[80,1024]{1,0:T(8,128)(2,1)S(1)} %get-tuple-element.278), channel_id=1, source_target_pairs={{0,2},{1,3},{2,4},{3,5},{4,6},{5,7},{6,0},{7,1},{8,10},{9,11},{10,... | collective-permute-start | bytes 491528 | tf_op jit(solution)/shard_map/ppermute | solution.py:31
  268.1 6.9 %collective-permute-start.33 = (bf16[80,1024]{1,0:T(8,128)(2,1)S(1)}, bf16[80,1024]{1,0:T(8,128)(2,1)S(1)}, u32[]{:S(2)}, u32[]{:S(2)}) collective-permute-start(bf16[80,1024]{1,0:T(8,128)(2,1)S(1)} %get-tuple-element.279), channel_id=1, source_target_pairs={{0,6},{1,7},{2,0},{3,1},{4,2},{5,3},{6,4},{7,5},{8,14},{9,15},{10,... | collective-permute-start | bytes 491528 | tf_op jit(solution)/shard_map/ppermute | solution.py:33
  270.0 8.1 %collective-permute-start.32 = (bf16[80,1024]{1,0:T(8,128)(2,1)S(1)}, bf16[80,1024]{1,0:T(8,128)(2,1)S(1)}, u32[]{:S(2)}, u32[]{:S(2)}) collective-permute-start(bf16[80,1024]{1,0:T(8,128)(2,1)S(1)} %get-tuple-element.280), channel_id=1, source_target_pairs={{0,4},{1,5},{2,6},{3,7},{4,0},{5,1},{6,2},{7,3},{8,12},{9,13},{10,... | collective-permute-start | bytes 491528 | tf_op jit(solution)/shard_map/ppermute | solution.py:32
  279.4 13.1 %collective-permute-start.36 = (bf16[80,1024]{1,0:T(8,128)(2,1)}, bf16[80,1024]{1,0:T(8,128)(2,1)}, u32[]{:S(2)}, u32[]{:S(2)}) collective-permute-start(bf16[80,1024]{1,0:T(8,128)(2,1)} %get-tuple-element.182), channel_id=1, source_target_pairs={{0,2},{1,3},{2,4},{3,5},{4,6},{5,7},{6,0},{7,1},{8,10},{9,11},{10,... | collective-permute-start | bytes 491528 | tf_op jit(solution)/shard_map/ppermute | solution.py:24
  279.9 12.5 %collective-permute-start.35 = (bf16[80,1024]{1,0:T(8,128)(2,1)}, bf16[80,1024]{1,0:T(8,128)(2,1)}, u32[]{:S(2)}, u32[]{:S(2)}) collective-permute-start(bf16[80,1024]{1,0:T(8,128)(2,1)} %get-tuple-element.182), channel_id=1, source_target_pairs={{0,4},{1,5},{2,6},{3,7},{4,0},{5,1},{6,2},{7,3},{8,12},{9,13},{10,... | collective-permute-start | bytes 491528 | tf_op jit(solution)/shard_map/ppermute | solution.py:23
  281.5 11.0 %collective-permute-start.34 = (bf16[80,1024]{1,0:T(8,128)(2,1)}, bf16[80,1024]{1,0:T(8,128)(2,1)}, u32[]{:S(2)}, u32[]{:S(2)}) collective-permute-start(bf16[80,1024]{1,0:T(8,128)(2,1)} %get-tuple-element.182), channel_id=1, source_target_pairs={{0,6},{1,7},{2,0},{3,1},{4,2},{5,3},{6,4},{7,5},{8,14},{9,15},{10,... | collective-permute-start | bytes 491528 | tf_op jit(solution)/shard_map/ppermute | solution.py:22
  305.3 13.7 %collective-permute-start.37 = (bf16[320,512]{0,1:T(8,128)(2,1)}, bf16[320,512]{0,1:T(8,128)(2,1)}, u32[]{:S(2)}, u32[]{:S(2)}) collective-permute-start(bf16[320,512]{0,1:T(8,128)(2,1)} %pad_maximum_fusion.29), channel_id=1, source_target_pairs={{0,1},{1,0},{2,3},{3,2},{4,5},{5,4},{6,7},{7,6},{8,9},{9,8},{10,11... | collective-permute-start | bytes 983048 | tf_op jit(solution)/shard_map/ppermute | solution.py:38
  324.0 16.9 %collective-permute-start.38 = (bf16[80,1024]{1,0:T(8,128)(2,1)S(1)}, bf16[80,1024]{1,0:T(8,128)(2,1)S(1)}, u32[]{:S(2)}, u32[]{:S(2)}) collective-permute-start(bf16[80,1024]{1,0:T(8,128)(2,1)S(1)} %get-tuple-element.275), channel_id=1, source_target_pairs={{0,2},{1,3},{2,4},{3,5},{4,6},{5,7},{6,0},{7,1},{8,10},{9,11},{10,... | collective-permute-start | bytes 491528 | tf_op jit(solution)/shard_map/ppermute | solution.py:31
  325.8 15.1 %collective-permute-start.40 = (bf16[80,1024]{1,0:T(8,128)(2,1)S(1)}, bf16[80,1024]{1,0:T(8,128)(2,1)S(1)}, u32[]{:S(2)}, u32[]{:S(2)}) collective-permute-start(bf16[80,1024]{1,0:T(8,128)(2,1)S(1)} %get-tuple-element.276), channel_id=1, source_target_pairs={{0,6},{1,7},{2,0},{3,1},{4,2},{5,3},{6,4},{7,5},{8,14},{9,15},{10,... | collective-permute-start | bytes 491528 | tf_op jit(solution)/shard_map/ppermute | solution.py:33
  326.9 14.0 %collective-permute-start.39 = (bf16[80,1024]{1,0:T(8,128)(2,1)S(1)}, bf16[80,1024]{1,0:T(8,128)(2,1)S(1)}, u32[]{:S(2)}, u32[]{:S(2)}) collective-permute-start(bf16[80,1024]{1,0:T(8,128)(2,1)S(1)} %get-tuple-element.277), channel_id=1, source_target_pairs={{0,4},{1,5},{2,6},{3,7},{4,0},{5,1},{6,2},{7,3},{8,12},{9,13},{10,... | collective-permute-start | bytes 491528 | tf_op jit(solution)/shard_map/ppermute | solution.py:32
  339.4 108.2 %collective-permute-start.63 = (bf16[1024,1536]{0,1:T(8,128)(2,1)}, bf16[1024,1536]{0,1:T(8,128)(2,1)}, u32[]{:S(2)}, u32[]{:S(2)}) collective-permute-start(bf16[1024,1536]{0,1:T(8,128)(2,1)} %maximum_maximum_fusion.1), channel_id=1, source_target_pairs={{0,1},{1,0},{2,3},{3,2},{4,5},{5,4},{6,7},{7,6},{8,9},{9,8},{10,11... | collective-permute-start | bytes 9437192 | tf_op jit(solution)/shard_map/ppermute | solution.py:38
  342.1 7.0 %collective-permute-start.43 = (bf16[80,1024]{1,0:T(8,128)(2,1)S(1)}, bf16[80,1024]{1,0:T(8,128)(2,1)S(1)}, u32[]{:S(2)}, u32[]{:S(2)}) collective-permute-start(bf16[80,1024]{1,0:T(8,128)(2,1)S(1)} %get-tuple-element.179), channel_id=1, source_target_pairs={{0,2},{1,3},{2,4},{3,5},{4,6},{5,7},{6,0},{7,1},{8,10},{9,11},{10,... | collective-permute-start | bytes 491528 | tf_op jit(solution)/shard_map/ppermute | solution.py:24
  342.1 11.0 %collective-permute-start.42 = (bf16[80,1024]{1,0:T(8,128)(2,1)S(1)}, bf16[80,1024]{1,0:T(8,128)(2,1)S(1)}, u32[]{:S(2)}, u32[]{:S(2)}) collective-permute-start(bf16[80,1024]{1,0:T(8,128)(2,1)S(1)} %get-tuple-element.179), channel_id=1, source_target_pairs={{0,4},{1,5},{2,6},{3,7},{4,0},{5,1},{6,2},{7,3},{8,12},{9,13},{10,... | collective-permute-start | bytes 491528 | tf_op jit(solution)/shard_map/ppermute | solution.py:23
  345.2 7.9 %collective-permute-start.41 = (bf16[80,1024]{1,0:T(8,128)(2,1)S(1)}, bf16[80,1024]{1,0:T(8,128)(2,1)S(1)}, u32[]{:S(2)}, u32[]{:S(2)}) collective-permute-start(bf16[80,1024]{1,0:T(8,128)(2,1)S(1)} %get-tuple-element.179), channel_id=1, source_target_pairs={{0,6},{1,7},{2,0},{3,1},{4,2},{5,3},{6,4},{7,5},{8,14},{9,15},{10,... | collective-permute-start | bytes 491528 | tf_op jit(solution)/shard_map/ppermute | solution.py:22
  364.6 16.3 %collective-permute-start.44 = (bf16[80,1024]{1,0:T(8,128)(2,1)}, bf16[80,1024]{1,0:T(8,128)(2,1)}, u32[]{:S(2)}, u32[]{:S(2)}) collective-permute-start(bf16[80,1024]{1,0:T(8,128)(2,1)} %get-tuple-element.272), channel_id=1, source_target_pairs={{0,2},{1,3},{2,4},{3,5},{4,6},{5,7},{6,0},{7,1},{8,10},{9,11},{10,... | collective-permute-start | bytes 491528 | tf_op jit(solution)/shard_map/ppermute | solution.py:31
  366.4 14.5 %collective-permute-start.46 = (bf16[80,1024]{1,0:T(8,128)(2,1)}, bf16[80,1024]{1,0:T(8,128)(2,1)}, u32[]{:S(2)}, u32[]{:S(2)}) collective-permute-start(bf16[80,1024]{1,0:T(8,128)(2,1)} %get-tuple-element.273), channel_id=1, source_target_pairs={{0,6},{1,7},{2,0},{3,1},{4,2},{5,3},{6,4},{7,5},{8,14},{9,15},{10,... | collective-permute-start | bytes 491528 | tf_op jit(solution)/shard_map/ppermute | solution.py:33
  367.4 13.5 %collective-permute-start.45 = (bf16[80,1024]{1,0:T(8,128)(2,1)}, bf16[80,1024]{1,0:T(8,128)(2,1)}, u32[]{:S(2)}, u32[]{:S(2)}) collective-permute-start(bf16[80,1024]{1,0:T(8,128)(2,1)} %get-tuple-element.274), channel_id=1, source_target_pairs={{0,4},{1,5},{2,6},{3,7},{4,0},{5,1},{6,2},{7,3},{8,12},{9,13},{10,... | collective-permute-start | bytes 491528 | tf_op jit(solution)/shard_map/ppermute | solution.py:32
  384.7 8.4 %collective-permute-start.48 = (bf16[80,1024]{1,0:T(8,128)(2,1)}, bf16[80,1024]{1,0:T(8,128)(2,1)}, u32[]{:S(2)}, u32[]{:S(2)}) collective-permute-start(bf16[80,1024]{1,0:T(8,128)(2,1)} %get-tuple-element.176), channel_id=1, source_target_pairs={{0,4},{1,5},{2,6},{3,7},{4,0},{5,1},{6,2},{7,3},{8,12},{9,13},{10,... | collective-permute-start | bytes 491528 | tf_op jit(solution)/shard_map/ppermute | solution.py:23
  420.7 18.5 %collective-permute-start.51 = (bf16[80,1024]{1,0:T(8,128)(2,1)}, bf16[80,1024]{1,0:T(8,128)(2,1)S(1)}, u32[]{:S(2)}, u32[]{:S(2)}) collective-permute-start(bf16[80,1024]{1,0:T(8,128)(2,1)} %get-tuple-element.269), channel_id=1, source_target_pairs={{0,2},{1,3},{2,4},{3,5},{4,6},{5,7},{6,0},{7,1},{8,10},{9,11},{10,... | collective-permute-start | bytes 491528 | tf_op jit(solution)/shard_map/ppermute | solution.py:31
  421.8 17.3 %collective-permute-start.53 = (bf16[80,1024]{1,0:T(8,128)(2,1)S(1)}, bf16[80,1024]{1,0:T(8,128)(2,1)S(1)}, u32[]{:S(2)}, u32[]{:S(2)}) collective-permute-start(bf16[80,1024]{1,0:T(8,128)(2,1)S(1)} %get-tuple-element.270), channel_id=1, source_target_pairs={{0,6},{1,7},{2,0},{3,1},{4,2},{5,3},{6,4},{7,5},{8,14},{9,15},{10,... | collective-permute-start | bytes 491528 | tf_op jit(solution)/shard_map/ppermute | solution.py:33
  423.3 15.8 %collective-permute-start.52 = (bf16[80,1024]{1,0:T(8,128)(2,1)S(1)}, bf16[80,1024]{1,0:T(8,128)(2,1)S(1)}, u32[]{:S(2)}, u32[]{:S(2)}) collective-permute-start(bf16[80,1024]{1,0:T(8,128)(2,1)S(1)} %get-tuple-element.271), channel_id=1, source_target_pairs={{0,4},{1,5},{2,6},{3,7},{4,0},{5,1},{6,2},{7,3},{8,12},{9,13},{10,... | collective-permute-start | bytes 491528 | tf_op jit(solution)/shard_map/ppermute | solution.py:32
  438.2 50.8 %collective-permute-start.58 = (bf16[1024,1536]{0,1:T(8,128)(2,1)}, bf16[1024,1536]{0,1:T(8,128)(2,1)}, u32[]{:S(2)}, u32[]{:S(2)}) collective-permute-start(bf16[1024,1536]{0,1:T(8,128)(2,1)} %maximum_maximum_fusion), channel_id=1, source_target_pairs={{0,1},{1,0},{2,3},{3,2},{4,5},{5,4},{6,7},{7,6},{8,9},{9,8},{10,11... | collective-permute-start | bytes 9437192 | tf_op jit(solution)/shard_map/ppermute | solution.py:38
  442.9 12.0 %all-to-all-start.2 = ((f32[16,12,128]{2,1,0:T(8,128)}), f32[16,12,128]{2,1,0:T(8,128)S(1)}, u32[]{:S(2)}, u32[]{:S(2)}) async-start(f32[16,12,128]{2,1,0:T(8,128)} %reshape.2214), calls=%async_computation.2 | async-start | bytes 262144 | tf_op jit(solution)/shard_map/all_to_all | solution.py:291
  455.6 53.5 %all-to-all-start.1 = ((bf16[16,64,1536]{2,1,0:T(8,128)(2,1)}), bf16[16,64,1536]{2,1,0:T(8,128)(2,1)S(1)}, u32[]{:S(2)}, u32[]{:S(2)}) async-start(bf16[16,64,1536]{2,1,0:T(8,128)(2,1)} %bitcast.413), calls=%async_computation.1 | async-start | bytes 6291456 | tf_op jit(solution)/shard_map/all_to_all | solution.py:258
  469.8 7.7 %collective-permute-start.21 = (bf16[80,1024]{1,0:T(8,128)(2,1)}, bf16[80,1024]{1,0:T(8,128)(2,1)}, u32[]{:S(2)}, u32[]{:S(2)}) collective-permute-start(bf16[80,1024]{1,0:T(8,128)(2,1)} %get-tuple-element.283), channel_id=1, source_target_pairs={{0,4},{1,5},{2,6},{3,7},{4,0},{5,1},{6,2},{7,3},{8,12},{9,13},{10,... | collective-permute-start | bytes 491528 | tf_op jit(solution)/shard_map/ppermute | solution.py:32
  479.5 34.1 %collective-permute-start.25 = (bf16[80,1024]{1,0:T(8,128)(2,1)}, bf16[80,1024]{1,0:T(8,128)(2,1)}, u32[]{:S(2)}, u32[]{:S(2)}) collective-permute-start(bf16[80,1024]{1,0:T(8,128)(2,1)} %get-tuple-element.191), channel_id=1, source_target_pairs={{0,2},{1,3},{2,4},{3,5},{4,6},{5,7},{6,0},{7,1},{8,10},{9,11},{10,... | collective-permute-start | bytes 491528 | tf_op jit(solution)/shard_map/ppermute | solution.py:24
  479.8 33.8 %collective-permute-start.24 = (bf16[80,1024]{1,0:T(8,128)(2,1)}, bf16[80,1024]{1,0:T(8,128)(2,1)}, u32[]{:S(2)}, u32[]{:S(2)}) collective-permute-start(bf16[80,1024]{1,0:T(8,128)(2,1)} %get-tuple-element.191), channel_id=1, source_target_pairs={{0,4},{1,5},{2,6},{3,7},{4,0},{5,1},{6,2},{7,3},{8,12},{9,13},{10,... | collective-permute-start | bytes 491528 | tf_op jit(solution)/shard_map/ppermute | solution.py:23
  482.2 31.4 %collective-permute-start.23 = (bf16[80,1024]{1,0:T(8,128)(2,1)}, bf16[80,1024]{1,0:T(8,128)(2,1)}, u32[]{:S(2)}, u32[]{:S(2)}) collective-permute-start(bf16[80,1024]{1,0:T(8,128)(2,1)} %get-tuple-element.191), channel_id=1, source_target_pairs={{0,6},{1,7},{2,0},{3,1},{4,2},{5,3},{6,4},{7,5},{8,14},{9,15},{10,... | collective-permute-start | bytes 491528 | tf_op jit(solution)/shard_map/ppermute | solution.py:22
  509.1 53.0 %all-to-all-start = ((bf16[16,64,1536]{2,1,0:T(8,128)(2,1)}), bf16[16,64,1536]{2,1,0:T(8,128)(2,1)}, u32[]{:S(2)}, u32[]{:S(2)}) async-start(bf16[16,64,1536]{2,1,0:T(8,128)(2,1)} %bitcast.412), calls=%async_computation | async-start | bytes 6291456 | tf_op jit(solution)/shard_map/all_to_all | solution.py:258
  515.7 15.1 %collective-permute-start.26 = (bf16[320,1024]{1,0:T(8,128)(2,1)}, bf16[320,1024]{1,0:T(8,128)(2,1)}, u32[]{:S(2)}, u32[]{:S(2)}) collective-permute-start(bf16[320,1024]{1,0:T(8,128)(2,1)} %pad_maximum_fusion.24), channel_id=1, source_target_pairs={{0,1},{1,0},{2,3},{3,2},{4,5},{5,4},{6,7},{7,6},{8,9},{9,8},{10,11... | collective-permute-start | bytes 1966088 | tf_op jit(solution)/shard_map/ppermute | solution.py:38
  529.6 8.9 %collective-permute-start.56 = (bf16[80,1024]{1,0:T(8,128)(2,1)}, bf16[80,1024]{1,0:T(8,128)(2,1)S(1)}, u32[]{:S(2)}, u32[]{:S(2)}) collective-permute-start(bf16[80,1024]{1,0:T(8,128)(2,1)} %get-tuple-element.185), channel_id=1, source_target_pairs={{0,2},{1,3},{2,4},{3,5},{4,6},{5,7},{6,0},{7,1},{8,10},{9,11},{10,... | collective-permute-start | bytes 491528 | tf_op jit(solution)/shard_map/ppermute | solution.py:24
  529.7 6.9 %collective-permute-start.71 = (f32[12,128]{1,0:T(8,128)S(1)}, f32[12,128]{1,0:T(8,128)S(1)}, u32[]{:S(2)}, u32[]{:S(2)}) collective-permute-start(f32[12,128]{1,0:T(8,128)S(1)} %add_add_fusion.1), channel_id=1, source_target_pairs={{0,1},{1,0},{2,3},{3,2},{4,5},{5,4},{6,7},{7,6},{8,9},{9,8},{10,11... | collective-permute-start | bytes 18440 | tf_op jit(solution)/shard_map/ppermute | solution.py:38
  532.8 10.7 %collective-permute-start.55 = (bf16[80,1024]{1,0:T(8,128)(2,1)}, bf16[80,1024]{1,0:T(8,128)(2,1)}, u32[]{:S(2)}, u32[]{:S(2)}) collective-permute-start(bf16[80,1024]{1,0:T(8,128)(2,1)} %get-tuple-element.185), channel_id=1, source_target_pairs={{0,4},{1,5},{2,6},{3,7},{4,0},{5,1},{6,2},{7,3},{8,12},{9,13},{10,... | collective-permute-start | bytes 491528 | tf_op jit(solution)/shard_map/ppermute | solution.py:23
  534.0 10.3 %collective-permute-start.54 = (bf16[80,1024]{1,0:T(8,128)(2,1)}, bf16[80,1024]{1,0:T(8,128)(2,1)}, u32[]{:S(2)}, u32[]{:S(2)}) collective-permute-start(bf16[80,1024]{1,0:T(8,128)(2,1)} %get-tuple-element.185), channel_id=1, source_target_pairs={{0,6},{1,7},{2,0},{3,1},{4,2},{5,3},{6,4},{7,5},{8,14},{9,15},{10,... | collective-permute-start | bytes 491528 | tf_op jit(solution)/shard_map/ppermute | solution.py:22
  536.0 11.5 %collective-permute-start.66 = (bf16[64,1536]{1,0:T(8,128)(2,1)S(1)}, bf16[64,1536]{1,0:T(8,128)(2,1)S(1)}, u32[]{:S(2)}, u32[]{:S(2)}) collective-permute-start(bf16[64,1536]{1,0:T(8,128)(2,1)S(1)} %reduce_sum.458), channel_id=1, source_target_pairs={{0,2},{1,3},{2,4},{3,5},{4,6},{5,7},{6,0},{7,1},{8,10},{9,11},{10,... | collective-permute-start | bytes 589832 | tf_op jit(solution)/shard_map/ppermute | solution.py:24
  536.6 12.1 %collective-permute-start.65 = (bf16[64,1536]{1,0:T(8,128)(2,1)S(1)}, bf16[64,1536]{1,0:T(8,128)(2,1)S(1)}, u32[]{:S(2)}, u32[]{:S(2)}) collective-permute-start(bf16[64,1536]{1,0:T(8,128)(2,1)S(1)} %reduce_sum.458), channel_id=1, source_target_pairs={{0,4},{1,5},{2,6},{3,7},{4,0},{5,1},{6,2},{7,3},{8,12},{9,13},{10,... | collective-permute-start | bytes 589832 | tf_op jit(solution)/shard_map/ppermute | solution.py:23
  538.5 14.3 %collective-permute-start.64 = (bf16[64,1536]{1,0:T(8,128)(2,1)S(1)}, bf16[64,1536]{1,0:T(8,128)(2,1)S(1)}, u32[]{:S(2)}, u32[]{:S(2)}) collective-permute-start(bf16[64,1536]{1,0:T(8,128)(2,1)S(1)} %reduce_sum.458), channel_id=1, source_target_pairs={{0,6},{1,7},{2,0},{3,1},{4,2},{5,3},{6,4},{7,5},{8,14},{9,15},{10,... | collective-permute-start | bytes 589832 | tf_op jit(solution)/shard_map/ppermute | solution.py:22
  546.2 13.6 %collective-permute-start.57 = (bf16[320,1024]{1,0:T(8,128)(2,1)}, bf16[320,1024]{1,0:T(8,128)(2,1)}, u32[]{:S(2)}, u32[]{:S(2)}) collective-permute-start(bf16[320,1024]{1,0:T(8,128)(2,1)} %pad_maximum_fusion.28), channel_id=1, source_target_pairs={{0,1},{1,0},{2,3},{3,2},{4,5},{5,4},{6,7},{7,6},{8,9},{9,8},{10,11... | collective-permute-start | bytes 1966088 | tf_op jit(solution)/shard_map/ppermute | solution.py:38
  554.6 13.1 %collective-permute-start.67 = (bf16[4,64,1536]{2,1,0:T(8,128)(2,1)S(1)}, bf16[4,64,1536]{2,1,0:T(8,128)(2,1)}, u32[]{:S(2)}, u32[]{:S(2)}) collective-permute-start(bf16[4,64,1536]{2,1,0:T(8,128)(2,1)S(1)} %get-tuple-element.260), channel_id=1, source_target_pairs={{0,1},{1,0},{2,3},{3,2},{4,5},{5,4},{6,7},{7,6},{8,9},{9,8},{10,11... | collective-permute-start | bytes 2359304 | tf_op jit(solution)/shard_map/ppermute | solution.py:38
  564.4 7.8 %collective-permute-start.61 = (bf16[64,1536]{1,0:T(8,128)(2,1)S(1)}, bf16[64,1536]{1,0:T(8,128)(2,1)S(1)}, u32[]{:S(2)}, u32[]{:S(2)}) collective-permute-start(bf16[64,1536]{1,0:T(8,128)(2,1)S(1)} %reduce_sum.457), channel_id=1, source_target_pairs={{0,2},{1,3},{2,4},{3,5},{4,6},{5,7},{6,0},{7,1},{8,10},{9,11},{10,... | collective-permute-start | bytes 589832 | tf_op jit(solution)/shard_map/ppermute | solution.py:24
  564.5 12.5 %collective-permute-start.60 = (bf16[64,1536]{1,0:T(8,128)(2,1)S(1)}, bf16[64,1536]{1,0:T(8,128)(2,1)S(1)}, u32[]{:S(2)}, u32[]{:S(2)}) collective-permute-start(bf16[64,1536]{1,0:T(8,128)(2,1)S(1)} %reduce_sum.457), channel_id=1, source_target_pairs={{0,4},{1,5},{2,6},{3,7},{4,0},{5,1},{6,2},{7,3},{8,12},{9,13},{10,... | collective-permute-start | bytes 589832 | tf_op jit(solution)/shard_map/ppermute | solution.py:23
  567.7 9.3 %collective-permute-start.59 = (bf16[64,1536]{1,0:T(8,128)(2,1)S(1)}, bf16[64,1536]{1,0:T(8,128)(2,1)S(1)}, u32[]{:S(2)}, u32[]{:S(2)}) collective-permute-start(bf16[64,1536]{1,0:T(8,128)(2,1)S(1)} %reduce_sum.457), channel_id=1, source_target_pairs={{0,6},{1,7},{2,0},{3,1},{4,2},{5,3},{6,4},{7,5},{8,14},{9,15},{10,... | collective-permute-start | bytes 589832 | tf_op jit(solution)/shard_map/ppermute | solution.py:22
  578.0 7.9 %collective-permute-start.62 = (bf16[4,64,1536]{2,1,0:T(8,128)(2,1)}, bf16[4,64,1536]{2,1,0:T(8,128)(2,1)}, u32[]{:S(2)}, u32[]{:S(2)}) collective-permute-start(bf16[4,64,1536]{2,1,0:T(8,128)(2,1)} %get-tuple-element.258), channel_id=1, source_target_pairs={{0,1},{1,0},{2,3},{3,2},{4,5},{5,4},{6,7},{7,6},{8,9},{9,8},{10,11... | collective-permute-start | bytes 2359304 | tf_op jit(solution)/shard_map/ppermute | solution.py:38
  (199 other events, 2044.1 us)
Sparse Core Ops, SparseCore 0:
  16.2 53.8 all-gather.4
  72.8 49.9 all-gather.2
